TPU v7x, 32 devices: a whole 2x2x4 slice. The times are simulated.
32 devices in a mesh: dp: 4 (over y, core), seq: 8 (over z, x).
Axes of the slice: x: 2, y: 2, z: 4, core: 2. Of those that a mesh axis runs over, the one named last changes fastest.
Arguments:
- tokens: bfloat16 [2, 8, 1024, 768], P(None, 'dp', 'seq'), may hold values from -6 to 6
- cotangent: bfloat16 [2, 8, 1024, 768], P(None, 'dp', 'seq'), may hold values from -6 to 6
- stretch_size: int32 [2, 8], P(None, 'dp'), may hold values from 128 to 1024, as said below
- w_value: bfloat16 [768, 1536], P(('dp', 'seq')), may hold values from -0.21875 to 0.21875
- w_base: bfloat16 [768, 3200], P(('dp', 'seq')), may hold values from -0.21875 to 0.21875
- w_out: bfloat16 [1536, 768], P(('dp', 'seq')), may hold values from -1.25 to 1.25
- w_up: bfloat16 [768, 1536], P(('dp', 'seq')), may hold values from -0.21875 to 0.21875
- w_down: bfloat16 [1536, 768], P(('dp', 'seq')), may hold values from -0.15625 to 0.15625
- ema_delta: bfloat16 [768, 16], P(('dp', 'seq')), may hold values from -8 to 0.1
- ema_alpha: bfloat16 [768, 16], P(('dp', 'seq')), may hold values from -9 to -1
- ema_beta: bfloat16 [768, 16], P(('dp', 'seq')), may hold values from -4 to 4
- ema_gamma: bfloat16 [768, 16], P(('dp', 'seq')), may hold values from -4 to 4
- ema_omega: bfloat16 [768], P(('dp', 'seq')), may hold values from -4 to 4
- first_gain: bfloat16 [768], P(('dp', 'seq')), may hold values from 0.5 to 1.5
- second_gain: bfloat16 [768], P(('dp', 'seq')), may hold values from 0.5 to 1.5
- query_gain: float32 [128], replicated, may hold values from -8 to 8
- query_bias: float32 [128], replicated, may hold values from -4 to 4
- key_gain: float32 [128], replicated, may hold values from -8 to 8
- relative_bias: float32 [32], replicated, may hold values from -4 to 4
Outputs:
- block_out: bfloat16 [2, 8, 1024, 768], P(None, 'dp', 'seq')
- grad_tokens: float32 [2, 8, 1024, 768], P(None, 'dp', 'seq')
- grad_w_value: float32 [768, 1536], P(('dp', 'seq'))
- grad_w_base: float32 [768, 3200], P(('dp', 'seq'))
- grad_w_out: float32 [1536, 768], P(('dp', 'seq'))
- grad_w_up: float32 [768, 1536], P(('dp', 'seq'))
- grad_w_down: float32 [1536, 768], P(('dp', 'seq'))
- grad_ema_delta: float32 [768, 16], P(('dp', 'seq'))
- grad_ema_alpha: float32 [768, 16], P(('dp', 'seq'))
- grad_ema_beta: float32 [768, 16], P(('dp', 'seq'))
- grad_ema_gamma: float32 [768, 16], P(('dp', 'seq'))
- grad_ema_omega: float32 [768], P(('dp', 'seq'))
- grad_first_gain: float32 [768], P(('dp', 'seq'))
- grad_second_gain: float32 [768], P(('dp', 'seq'))
- grad_query_gain: float32 [128], replicated
- grad_query_bias: float32 [128], replicated
- grad_key_gain: float32 [128], replicated
- grad_relative_bias: float32 [32], replicated
Inputs may be any that keep to these rules, and one draw needn't show every extreme that they name: `stretch_size`: in each micro-batch, exactly one of the 2 sequences of each index of dp has the value 1024; the others have 128.
All inputs are finite; a program needn't handle non-finite values.
Results may differ from a plain program's by a relative error of at most 0.033.
The roundings to bfloat16 on the way count: a program that leaves them out, or rounds other values in their place, can miss the bound.
Values may be sent and summed in bfloat16 or wider, within the bound.
A program may use at most 384 MiB of HBM per device.

v0:
```python
from functools import reduce

import jax
import jax.numpy as jnp
import numpy as np
from jax import lax
from jax.sharding import PartitionSpec as P

EMA_BLOCK = 64


highest = lax.Precision.HIGHEST
epsilon = 1e-05
masked_fill = -1e30


def carried_in(value, axis, join, neutral, backward):
    count, mine = (lax.axis_size(axis), lax.axis_index(axis))
    pieces = jax.tree.map(lambda part: lax.all_gather(part, axis), value)
    if backward:
        pieces = jax.tree.map(lambda part: part[::-1], pieces)
        mine = count - 1 - mine
    so_far = jax.tree.map(
        lambda part, zero: jnp.full_like(part, 0) + jnp.asarray(zero, part.dtype), value, neutral
    )

    def hop(position, so_far):
        longer = join(so_far, jax.tree.map(lambda part: part[position], pieces))
        return jax.tree.map(lambda new, old: jnp.where(position < mine, new, old), longer, so_far)

    return lax.fori_loop(0, count - 1, hop, so_far)


def bucket_edges(bucket_count):
    edge_list = [0]
    middle = bucket_count // 2
    for number in range(1, bucket_count):
        edge_list.append(number if number < middle else int(middle * 2 ** ((number - middle) / 2)))
    return np.array(edge_list, np.int32)


def silu_slope(values):
    gate_value = jax.nn.sigmoid(values)
    return gate_value * (1.0 + values * (1.0 - gate_value))


def normalize(seq_rows):
    centered = seq_rows - jnp.mean(seq_rows, axis=-1, keepdims=True)
    inverse = lax.rsqrt(jnp.mean(centered * centered, axis=-1, keepdims=True) + epsilon)
    return (centered * inverse, inverse)


def normalize_back(grad_scaled, unit_rows, inverse):
    return inverse * (
        grad_scaled
        - jnp.mean(grad_scaled, axis=-1, keepdims=True)
        - unit_rows * jnp.mean(grad_scaled * unit_rows, axis=-1, keepdims=True)
    )


def ema_tables(params, ema_steps):
    delta_raw, alpha_raw, beta_raw, gamma_raw = (params[0], params[1], params[2], params[3])
    leak_rate = jax.nn.sigmoid(delta_raw)
    log_decay = jnp.log(1.0 - leak_rate * jax.nn.sigmoid(alpha_raw))
    drive_gain = leak_rate * beta_raw
    readout = gamma_raw * gamma_raw.shape[1] ** (-0.5)
    offsets = jnp.arange(ema_steps, dtype=jnp.float32)
    powers = jnp.exp((offsets + 1.0)[:, None, None] * log_decay) * readout
    inject = jnp.exp((ema_steps - 1.0 - offsets)[:, None, None] * log_decay) * drive_gain
    kernel = jnp.einsum(
        "tdh,dh->td",
        jnp.exp(offsets[:, None, None] * log_decay),
        readout * drive_gain,
        precision=highest,
    )
    lag_grid = offsets[:, None] - offsets[None, :]
    onehot = (lag_grid[:, :, None] == offsets[None, None, :]).astype(jnp.float32)
    toeplitz = jnp.einsum("rst,td->rsd", onehot, kernel, precision=highest)
    return (powers, inject, toeplitz, jnp.exp(ema_steps * log_decay))


def ema_step(tables, ema_state, block_input):
    powers, inject, toeplitz, block_decay = tables
    output = jnp.einsum("rsd,...sd->...rd", toeplitz, block_input, precision=highest)
    output = output + jnp.einsum("rdh,...dh->...rd", powers, ema_state, precision=highest)
    ema_state = block_decay * ema_state + jnp.einsum(
        "rdh,...rd->...dh", inject, block_input, precision=highest
    )
    return (ema_state, output)


def carry_terms(params, row_total):
    leak_rate = jax.nn.sigmoid(params[0])
    log_decay = jnp.log(1.0 - leak_rate * jax.nn.sigmoid(params[1]))
    readout = params[3] * params[3].shape[1] ** (-0.5)
    spans = jnp.arange(row_total, dtype=jnp.float32)
    reach_table = jnp.exp((spans + 1.0)[:, None, None] * log_decay) * readout
    return (reach_table, jnp.exp(row_total * log_decay))


def ema_local(seq_rows, incoming, params, ema_steps):
    tables = ema_tables(params, ema_steps)
    item_count, row_total, model_width = seq_rows.shape
    blocks = jnp.moveaxis(
        seq_rows.reshape(item_count, row_total // ema_steps, ema_steps, model_width), 1, 0
    )

    def advance(ema_state, block_input):
        return ema_step(tables, ema_state, block_input)

    end_states, outputs = lax.scan(advance, jnp.zeros(incoming.shape, jnp.float32), blocks)
    local_out = jnp.moveaxis(outputs, 0, 1).reshape(seq_rows.shape)
    reach_table, device_decay = carry_terms(params, row_total)
    carried = jnp.einsum("tdh,sdh->std", reach_table, incoming, precision=highest)
    return (local_out + carried + params[4] * seq_rows, end_states + device_decay * incoming)


def chain_combine(earlier, latter):
    return (latter[0] * earlier[0], latter[1] + latter[0] * earlier[1])


def block_parts(
    query_rows, key_rows, query_pos, key_pos, stretch_width, relative_bias, edge_values
):
    lag_grid = query_pos[:, None] - key_pos[None, :]
    allowed = (lag_grid >= 0) & (
        query_pos[:, None] // stretch_width == key_pos[None, :] // stretch_width
    )
    climbs = (lag_grid[:, :, None] >= edge_values[None, None, :]).astype(jnp.float32)
    bias_steps = relative_bias[1:] - relative_bias[:-1]
    bias_grid = relative_bias[0] + jnp.einsum("qkb,b->qk", climbs, bias_steps, precision=highest)
    scores = jnp.dot(query_rows, key_rows.T, preferred_element_type=jnp.float32) * query_rows.shape[
        1
    ] ** (-0.5)
    return (scores + bias_grid, allowed, climbs)


def attend_forward(
    queries, keyvals, key_base, query_base, stretch_width, block_rows, block_count, relative_bias
):
    query_count, z_width = queries.shape
    v_width = keyvals.shape[1] - z_width
    edge_values = jnp.asarray(bucket_edges(relative_bias.shape[0])[1:])
    query_pos = query_base + jnp.arange(query_count, dtype=jnp.int32)

    def scores_at(block_index):
        key_start = block_index * block_rows
        key_piece = lax.dynamic_slice_in_dim(keyvals, key_start, block_rows, 0)
        key_pos = key_base + key_start + jnp.arange(block_rows, dtype=jnp.int32)
        scores, allowed, climbs = block_parts(
            queries,
            key_piece[:, :z_width],
            query_pos,
            key_pos,
            stretch_width,
            relative_bias,
            edge_values,
        )
        return (key_piece, scores, allowed)

    def gather_stats(block_index, loop_state):
        running, exp_total = loop_state
        key_piece, scores, allowed = scores_at(block_index)
        masked = jnp.where(allowed, scores, masked_fill)
        newmax = jnp.maximum(running, jnp.max(masked, axis=1))
        exp_total = exp_total * jnp.exp(running - newmax) + jnp.sum(
            jnp.where(allowed, jnp.exp(masked - newmax[:, None]), 0.0), axis=1
        )
        return (newmax, exp_total)

    initial = (
        jnp.full((query_count,), masked_fill, jnp.float32),
        jnp.zeros((query_count,), jnp.float32),
    )
    running, exp_total = lax.fori_loop(0, block_count, gather_stats, initial)
    log_total = running + jnp.log(exp_total)

    def accumulate(block_index, accumulated):
        key_piece, scores, allowed = scores_at(block_index)
        weights = jnp.where(allowed, jnp.exp(scores - log_total[:, None]), 0.0).astype(jnp.bfloat16)
        return accumulated + jnp.dot(
            weights, key_piece[:, z_width:], preferred_element_type=jnp.float32
        )

    attended = lax.fori_loop(
        0, block_count, accumulate, jnp.zeros((query_count, v_width), jnp.float32)
    )
    return (attended, log_total)


def attend_backward(
    queries,
    keyvals,
    key_base,
    query_base,
    stretch_width,
    block_rows,
    block_count,
    relative_bias,
    log_total,
    row_delta,
    grad_att,
    want_keys,
):
    query_count, z_width = queries.shape
    score_scale = z_width ** (-0.5)
    edge_values = jnp.asarray(bucket_edges(relative_bias.shape[0])[1:])
    query_pos = query_base + jnp.arange(query_count, dtype=jnp.int32)

    def step_back(block_index, loop_state):
        key_start = block_index * block_rows
        key_piece = lax.dynamic_slice_in_dim(keyvals, key_start, block_rows, 0)
        key_pos = key_base + key_start + jnp.arange(block_rows, dtype=jnp.int32)
        scores, allowed, climbs = block_parts(
            queries,
            key_piece[:, :z_width],
            query_pos,
            key_pos,
            stretch_width,
            relative_bias,
            edge_values,
        )
        weights = jnp.where(allowed, jnp.exp(scores - log_total[:, None]), 0.0)
        weights_low = weights.astype(jnp.bfloat16)
        grad_weights = jnp.dot(
            grad_att, key_piece[:, z_width:].T, preferred_element_type=jnp.float32
        )
        score_sums = weights * (grad_weights - row_delta[:, None])
        grad_scores = score_sums.astype(jnp.bfloat16)
        grad_queries = (
            loop_state[0]
            + jnp.dot(grad_scores, key_piece[:, :z_width], preferred_element_type=jnp.float32)
            * score_scale
        )
        bucket_sums = loop_state[1] + jnp.concatenate(
            [
                jnp.sum(score_sums)[None],
                jnp.einsum("qk,qkb->b", score_sums, climbs, precision=highest),
            ]
        )
        if want_keys:
            grad_keys = (
                jnp.dot(grad_scores.T, queries, preferred_element_type=jnp.float32) * score_scale
            )
            grad_values = jnp.dot(weights_low.T, grad_att, preferred_element_type=jnp.float32)
            buffer = jnp.concatenate([grad_keys, grad_values], 1)
            return (grad_queries, bucket_sums, buffer)
        return (grad_queries, bucket_sums)

    initial = (
        jnp.zeros((query_count, z_width), jnp.float32),
        jnp.zeros(relative_bias.shape, jnp.float32),
    )
    if want_keys:
        initial = initial + (jnp.zeros(keyvals.shape, jnp.float32),)
    result = lax.fori_loop(0, block_count, step_back, initial)
    if want_keys:
        return result
    return (result[0], result[1], None)


def keys_backward(
    all_queries,
    all_att,
    all_lse,
    all_delta,
    local_keyvals,
    key_base,
    stretch_width,
    block_rows,
    relative_bias,
):
    key_count, kv_width = local_keyvals.shape
    z_width = all_queries.shape[1]
    score_scale = z_width ** (-0.5)
    edge_values = jnp.asarray(bucket_edges(relative_bias.shape[0])[1:])
    key_pos = key_base + jnp.arange(key_count, dtype=jnp.int32)
    key_rows = local_keyvals[:, :z_width]
    value_rows = local_keyvals[:, z_width:]

    def step_keys(block_index, grads):
        query_start = block_index * block_rows
        query_rows = lax.dynamic_slice_in_dim(all_queries, query_start, block_rows, 0)
        att_rows = lax.dynamic_slice_in_dim(all_att, query_start, block_rows, 0)
        lse_rows = lax.dynamic_slice_in_dim(all_lse, query_start, block_rows, 0)
        delta_rows = lax.dynamic_slice_in_dim(all_delta, query_start, block_rows, 0)
        query_pos = query_start + jnp.arange(block_rows, dtype=jnp.int32)
        scores, allowed, climbs = block_parts(
            query_rows, key_rows, query_pos, key_pos, stretch_width, relative_bias, edge_values
        )
        weights = jnp.where(allowed, jnp.exp(scores - lse_rows[:, None]), 0.0)
        weights_low = weights.astype(jnp.bfloat16)
        grad_weights = jnp.dot(att_rows, value_rows.T, preferred_element_type=jnp.float32)
        grad_scores = (weights * (grad_weights - delta_rows[:, None])).astype(jnp.bfloat16)
        grad_keys = (
            jnp.dot(grad_scores.T, query_rows, preferred_element_type=jnp.float32) * score_scale
        )
        grad_values = jnp.dot(weights_low.T, att_rows, preferred_element_type=jnp.float32)
        return grads + jnp.concatenate([grad_keys, grad_values], 1)

    first_block = key_base // block_rows
    last_block = all_queries.shape[0] // block_rows
    return lax.fori_loop(
        first_block, last_block, step_keys, jnp.zeros((key_count, kv_width), jnp.float32)
    )


def pick_item(stacked, chosen):
    return lax.dynamic_index_in_dim(stacked, chosen, 0, keepdims=False)


def place_items(full_part, other_parts, full_index, item_count):
    placed = []
    for member in range(item_count):
        below_part = other_parts[member] if member < item_count - 1 else full_part
        above_part = other_parts[member - 1] if member >= 1 else full_part
        placed.append(
            jnp.where(
                member == full_index,
                full_part,
                jnp.where(member < full_index, below_part, above_part),
            )
        )
    return jnp.stack(placed)


def forward_micro(token_block, widths, weights_all, small_params, length, position):
    mat_value, mat_base, mat_out, mat_up, mat_down = weights_all[:5]
    ema_params = tuple((member.astype(jnp.float32) for member in weights_all[5:10]))
    gain_first = weights_all[10].astype(jnp.float32)
    gain_second = weights_all[11].astype(jnp.float32)
    query_gain, query_bias, key_gain, relative_bias = small_params
    item_count, seq_len, model_width = token_block.shape
    z_width = query_gain.shape[0]
    v_width = mat_value.shape[1]
    token_rows = token_block.reshape(-1, model_width)
    token_wide = token_rows.astype(jnp.float32)
    value_pre = jnp.dot(token_rows, mat_value, preferred_element_type=jnp.float32)
    values_low = jax.nn.silu(value_pre).astype(jnp.bfloat16)
    start_state = jnp.zeros((item_count,) + ema_params[0].shape, jnp.float32)
    ema_first, end_states = ema_local(
        token_wide.reshape(token_block.shape), start_state, ema_params, EMA_BLOCK
    )
    reach_table, device_decay = carry_terms(ema_params, seq_len)
    incoming = carried_in(
        (device_decay, end_states),
        "seq",
        chain_combine,
        (jnp.ones_like(device_decay), jnp.zeros_like(end_states)),
        False,
    )[1]
    ema_out = (
        ema_first + jnp.einsum("tdh,sdh->std", reach_table, incoming, precision=highest)
    ).reshape(-1, model_width)
    mixed_low = jax.nn.silu(ema_out).astype(jnp.bfloat16)
    base_out = jnp.dot(mixed_low, mat_base, preferred_element_type=jnp.float32)
    z_pre = base_out[:, :z_width]
    reset_pre = base_out[:, z_width : z_width + v_width]
    cand_pre = base_out[:, z_width + v_width : z_width + v_width + model_width]
    update_pre = base_out[:, z_width + v_width + model_width :]
    shared = jax.nn.silu(z_pre)
    queries_low = (shared * query_gain + query_bias).astype(jnp.bfloat16)
    keys_low = (shared * key_gain).astype(jnp.bfloat16)
    keyvals = jnp.concatenate([keys_low, values_low], 1).reshape(
        item_count, seq_len, z_width + v_width
    )
    query_items = queries_low.reshape(item_count, seq_len, z_width)
    full_index = jnp.sum(
        jnp.arange(item_count, dtype=jnp.int32) * (widths == length).astype(jnp.int32)
    )
    full_keyvals = pick_item(keyvals, full_index)
    all_keys = lax.all_gather(full_keyvals, "seq", axis=0, tiled=True)
    block_rows = min(512, length)
    block_count = ((position + 1) * seq_len + block_rows - 1) // block_rows
    local_base = position * seq_len
    full_att, full_lse = attend_forward(
        pick_item(query_items, full_index),
        all_keys,
        0,
        local_base,
        length,
        block_rows,
        block_count,
        relative_bias,
    )
    member = 0
    chosen = member + (member >= full_index).astype(jnp.int32)
    part_att, part_lse = attend_forward(
        pick_item(query_items, chosen),
        pick_item(keyvals, chosen),
        local_base,
        local_base,
        pick_item(widths, chosen),
        seq_len,
        1,
        relative_bias,
    )
    other_att = [part_att]
    other_lse = [part_lse]
    attended = place_items(full_att, other_att, full_index, item_count).reshape(-1, v_width)
    log_totals = place_items(full_lse, other_lse, full_index, item_count)
    reset_gate = jax.nn.silu(reset_pre)
    update = jax.nn.sigmoid(update_pre)
    gated_low = (attended * reset_gate).astype(jnp.bfloat16)
    cand_in = cand_pre + jnp.dot(gated_low, mat_out, preferred_element_type=jnp.float32)
    candidate = jax.nn.silu(cand_in)
    first_sum = token_wide + update * (candidate - token_wide)
    unit_first, inverse_first = normalize(first_sum)
    normed = unit_first * gain_first
    normed_low = normed.astype(jnp.bfloat16)
    hidden_pre = jnp.dot(normed_low, mat_up, preferred_element_type=jnp.float32)
    hidden_low = jax.nn.silu(hidden_pre).astype(jnp.bfloat16)
    second_sum = normed + jnp.dot(hidden_low, mat_down, preferred_element_type=jnp.float32)
    unit_second, inverse_second = normalize(second_sum)
    output = (unit_second * gain_second).astype(jnp.bfloat16).reshape(token_block.shape)
    return {
        "value_pre": value_pre,
        "ema_out": ema_out,
        "incoming": incoming,
        "mixed_low": mixed_low,
        "z_pre": z_pre,
        "reset_pre": reset_pre,
        "shared": shared,
        "query_items": query_items,
        "keyvals": keyvals,
        "full_index": full_index,
        "full_keyvals": full_keyvals,
        "all_keys": all_keys,
        "widths": widths,
        "attended": attended,
        "log_totals": log_totals,
        "update": update,
        "gated_low": gated_low,
        "cand_in": cand_in,
        "candidate": candidate,
        "unit_first": unit_first,
        "inverse_first": inverse_first,
        "normed_low": normed_low,
        "hidden_pre": hidden_pre,
        "hidden_low": hidden_low,
        "unit_second": unit_second,
        "inverse_second": inverse_second,
        "output": output,
    }


def backward_micro(
    stored, token_block, grad_out, weights_all, small_params, key_source, length, position
):
    mat_value, mat_base, mat_out, mat_up, mat_down = weights_all[:5]
    ema_params = tuple((member.astype(jnp.float32) for member in weights_all[5:10]))
    gain_first = weights_all[10].astype(jnp.float32)
    gain_second = weights_all[11].astype(jnp.float32)
    query_gain, query_bias, key_gain, relative_bias = small_params
    item_count, seq_len, model_width = token_block.shape
    z_width = query_gain.shape[0]
    v_width = mat_value.shape[1]
    token_rows = token_block.reshape(-1, model_width)
    token_wide = token_rows.astype(jnp.float32)
    grad_rows = grad_out.reshape(-1, model_width).astype(jnp.float32)
    grad_gain_second = jnp.sum(grad_rows * stored["unit_second"], axis=0)
    grad_second = normalize_back(
        grad_rows * gain_second, stored["unit_second"], stored["inverse_second"]
    )
    branch_low = grad_second.astype(jnp.bfloat16)
    grad_mat_down = jnp.dot(stored["hidden_low"].T, branch_low, preferred_element_type=jnp.float32)
    hidden_grad = (
        jnp.dot(branch_low, mat_down.T, preferred_element_type=jnp.float32)
        * silu_slope(stored["hidden_pre"])
    ).astype(jnp.bfloat16)
    grad_mat_up = jnp.dot(stored["normed_low"].T, hidden_grad, preferred_element_type=jnp.float32)
    grad_normed = grad_second + jnp.dot(hidden_grad, mat_up.T, preferred_element_type=jnp.float32)
    grad_gain_first = jnp.sum(grad_normed * stored["unit_first"], axis=0)
    grad_first = normalize_back(
        grad_normed * gain_first, stored["unit_first"], stored["inverse_first"]
    )
    update = stored["update"]
    cand_low = (grad_first * update * silu_slope(stored["cand_in"])).astype(jnp.bfloat16)
    grad_mat_out = jnp.dot(stored["gated_low"].T, cand_low, preferred_element_type=jnp.float32)
    grad_gated = jnp.dot(cand_low, mat_out.T, preferred_element_type=jnp.float32)
    reset_pre = stored["reset_pre"]
    attended = stored["attended"]
    att_low = (grad_gated * jax.nn.silu(reset_pre)).astype(jnp.bfloat16)
    grad_reset_pre = grad_gated * attended * silu_slope(reset_pre)
    grad_update_pre = grad_first * (stored["candidate"] - token_wide) * update * (1.0 - update)
    row_delta = jnp.sum(att_low.astype(jnp.float32) * attended, axis=1).reshape(item_count, seq_len)
    att_items = att_low.reshape(item_count, seq_len, v_width)
    query_items = stored["query_items"]
    keyvals = stored["keyvals"]
    log_totals = stored["log_totals"]
    widths = stored["widths"]
    full_index = stored["full_index"]
    block_rows = min(512, length)
    block_count = ((position + 1) * seq_len + block_rows - 1) // block_rows
    local_base = position * seq_len
    full_queries = pick_item(query_items, full_index)
    full_lse = pick_item(log_totals, full_index)
    full_delta = pick_item(row_delta, full_index)
    full_att_grad = pick_item(att_items, full_index)
    full_grad_q, full_sums, unused_buffer = attend_backward(
        full_queries,
        key_source,
        0,
        local_base,
        length,
        block_rows,
        block_count,
        relative_bias,
        full_lse,
        full_delta,
        full_att_grad,
        False,
    )
    all_queries, all_att = (
        lax.all_gather(full_queries, "seq", axis=0, tiled=True),
        lax.all_gather(full_att_grad, "seq", axis=0, tiled=True),
    )
    all_lse, all_delta = (
        lax.all_gather(full_lse, "seq", axis=0, tiled=True),
        lax.all_gather(full_delta, "seq", axis=0, tiled=True),
    )
    full_grad_kv = keys_backward(
        all_queries,
        all_att,
        all_lse,
        all_delta,
        stored["full_keyvals"],
        local_base,
        length,
        block_rows,
        relative_bias,
    )
    bucket_sums = full_sums
    member = 0
    chosen = member + (member >= full_index).astype(jnp.int32)
    part_q, part_sums, part_kv = attend_backward(
        pick_item(query_items, chosen),
        pick_item(keyvals, chosen),
        local_base,
        local_base,
        pick_item(widths, chosen),
        seq_len,
        1,
        relative_bias,
        pick_item(log_totals, chosen),
        pick_item(row_delta, chosen),
        pick_item(att_items, chosen),
        True,
    )
    other_q = [part_q]
    other_kv = [part_kv]
    bucket_sums = bucket_sums + part_sums
    grad_queries = place_items(full_grad_q, other_q, full_index, item_count).reshape(-1, z_width)
    grad_kv = place_items(full_grad_kv, other_kv, full_index, item_count).reshape(
        -1, z_width + v_width
    )
    grad_keys = grad_kv[:, :z_width]
    grad_values = grad_kv[:, z_width:]
    shared = stored["shared"]
    grad_query_gain = jnp.sum(grad_queries * shared, axis=0)
    grad_query_bias = jnp.sum(grad_queries, axis=0)
    grad_key_gain = jnp.sum(grad_keys * shared, axis=0)
    grad_relative = bucket_sums - jnp.concatenate([bucket_sums[1:], jnp.zeros((1,), jnp.float32)])
    grad_z_pre = (grad_queries * query_gain + grad_keys * key_gain) * silu_slope(stored["z_pre"])
    base_low = jnp.concatenate(
        [grad_z_pre, grad_reset_pre, cand_low.astype(jnp.float32), grad_update_pre], 1
    ).astype(jnp.bfloat16)
    grad_mat_base = jnp.dot(stored["mixed_low"].T, base_low, preferred_element_type=jnp.float32)
    grad_mixed = jnp.dot(base_low, mat_base.T, preferred_element_type=jnp.float32)
    grad_ema_out = (grad_mixed * silu_slope(stored["ema_out"])).reshape(
        item_count, seq_len, model_width
    )
    reach_table, device_decay = carry_terms(ema_params, seq_len)
    local_grad = jnp.einsum("tdh,std->sdh", reach_table, grad_ema_out, precision=highest)
    from_later = carried_in(
        (device_decay, local_grad),
        "seq",
        chain_combine,
        (jnp.ones_like(device_decay), jnp.zeros_like(local_grad)),
        True,
    )[1]
    incoming = stored["incoming"]

    def ema_again(seq_rows, ema_values):
        return ema_local(seq_rows, incoming, ema_values, EMA_BLOCK)

    unused_out, pullback = jax.vjp(ema_again, token_wide.reshape(token_block.shape), ema_params)
    grad_rows_ema, grad_ema = pullback((grad_ema_out, from_later))
    value_low = (grad_values * silu_slope(stored["value_pre"])).astype(jnp.bfloat16)
    grad_mat_value = jnp.dot(token_rows.T, value_low, preferred_element_type=jnp.float32)
    grad_tokens = (
        grad_first * (1.0 - update)
        + grad_rows_ema.reshape(-1, model_width)
        + jnp.dot(value_low, mat_value.T, preferred_element_type=jnp.float32)
    )
    full_grads = (
        grad_mat_value,
        grad_mat_base,
        grad_mat_out,
        grad_mat_up,
        grad_mat_down,
        grad_ema[0],
        grad_ema[1],
        grad_ema[2],
        grad_ema[3],
        grad_ema[4],
        grad_gain_first,
        grad_gain_second,
    )
    small_grads = (grad_query_gain, grad_query_bias, grad_key_gain, grad_relative)
    return (grad_tokens.reshape(token_block.shape), full_grads, small_grads)


def shards(
    tokens,
    cotangent,
    stretch_size,
    w_value,
    w_base,
    w_out,
    w_up,
    w_down,
    ema_delta,
    ema_alpha,
    ema_beta,
    ema_gamma,
    ema_omega,
    first_gain,
    second_gain,
    query_gain,
    query_bias,
    key_gain,
    relative_bias,
):
    micro_count, item_count, seq_len, model_width = tokens.shape
    position = lax.axis_index("seq")
    length = seq_len * lax.axis_size("seq")
    small_params = (query_gain, query_bias, key_gain, relative_bias)
    saved_list = []
    for batch_index in range(micro_count):
        weights_fwd = (
            lax.all_gather(w_value, ("dp", "seq"), axis=0, tiled=True),
            lax.all_gather(w_base, ("dp", "seq"), axis=0, tiled=True),
            lax.all_gather(w_out, ("dp", "seq"), axis=0, tiled=True),
            lax.all_gather(w_up, ("dp", "seq"), axis=0, tiled=True),
            lax.all_gather(w_down, ("dp", "seq"), axis=0, tiled=True),
            lax.all_gather(ema_delta, ("dp", "seq"), axis=0, tiled=True),
            lax.all_gather(ema_alpha, ("dp", "seq"), axis=0, tiled=True),
            lax.all_gather(ema_beta, ("dp", "seq"), axis=0, tiled=True),
            lax.all_gather(ema_gamma, ("dp", "seq"), axis=0, tiled=True),
            lax.all_gather(ema_omega, ("dp", "seq"), axis=0, tiled=True),
            lax.all_gather(first_gain, ("dp", "seq"), axis=0, tiled=True),
            lax.all_gather(second_gain, ("dp", "seq"), axis=0, tiled=True),
        )
        saved_list.append(
            forward_micro(
                tokens[batch_index],
                stretch_size[batch_index],
                weights_fwd,
                small_params,
                length,
                position,
            )
        )
    block_out = jnp.stack([stored["output"] for stored in saved_list])
    grad_blocks = [None] * micro_count
    collected = []
    collected_small = []
    for batch_index in range(micro_count - 1, -1, -1):
        weights_bwd = (
            lax.all_gather(w_value, ("dp", "seq"), axis=0, tiled=True),
            lax.all_gather(w_base, ("dp", "seq"), axis=0, tiled=True),
            lax.all_gather(w_out, ("dp", "seq"), axis=0, tiled=True),
            lax.all_gather(w_up, ("dp", "seq"), axis=0, tiled=True),
            lax.all_gather(w_down, ("dp", "seq"), axis=0, tiled=True),
            lax.all_gather(ema_delta, ("dp", "seq"), axis=0, tiled=True),
            lax.all_gather(ema_alpha, ("dp", "seq"), axis=0, tiled=True),
            lax.all_gather(ema_beta, ("dp", "seq"), axis=0, tiled=True),
            lax.all_gather(ema_gamma, ("dp", "seq"), axis=0, tiled=True),
            lax.all_gather(ema_omega, ("dp", "seq"), axis=0, tiled=True),
            lax.all_gather(first_gain, ("dp", "seq"), axis=0, tiled=True),
            lax.all_gather(second_gain, ("dp", "seq"), axis=0, tiled=True),
        )
        stored = saved_list[batch_index]
        key_source = lax.all_gather(stored["full_keyvals"], "seq", axis=0, tiled=True)
        grad_block, full_grads, small_grads = backward_micro(
            stored,
            tokens[batch_index],
            cotangent[batch_index],
            weights_bwd,
            small_params,
            key_source,
            length,
            position,
        )
        grad_blocks[batch_index] = grad_block
        collected_small.append(small_grads)
        collected.append(
            (
                lax.psum_scatter(full_grads[0], ("dp", "seq"), scatter_dimension=0, tiled=True),
                lax.psum_scatter(full_grads[1], ("dp", "seq"), scatter_dimension=0, tiled=True),
                lax.psum_scatter(full_grads[2], ("dp", "seq"), scatter_dimension=0, tiled=True),
                lax.psum_scatter(full_grads[3], ("dp", "seq"), scatter_dimension=0, tiled=True),
                lax.psum_scatter(full_grads[4], ("dp", "seq"), scatter_dimension=0, tiled=True),
                lax.psum_scatter(full_grads[5], ("dp", "seq"), scatter_dimension=0, tiled=True),
                lax.psum_scatter(full_grads[6], ("dp", "seq"), scatter_dimension=0, tiled=True),
                lax.psum_scatter(full_grads[7], ("dp", "seq"), scatter_dimension=0, tiled=True),
                lax.psum_scatter(full_grads[8], ("dp", "seq"), scatter_dimension=0, tiled=True),
                lax.psum_scatter(full_grads[9], ("dp", "seq"), scatter_dimension=0, tiled=True),
                lax.psum_scatter(full_grads[10], ("dp", "seq"), scatter_dimension=0, tiled=True),
                lax.psum_scatter(full_grads[11], ("dp", "seq"), scatter_dimension=0, tiled=True),
            )
        )
    merged = tuple(
        (
            reduce(jnp.add, [entry_grads[member] for entry_grads in collected])
            for member in range(12)
        )
    )
    small_local = tuple(
        (
            reduce(jnp.add, [entry_grads[member] for entry_grads in collected_small])
            for member in range(4)
        )
    )
    small_total = lax.psum(
        (small_local[0], small_local[1], small_local[2], small_local[3]), ("dp", "seq")
    )
    grad_tokens = jnp.stack(grad_blocks)
    return (
        block_out,
        grad_tokens,
        merged[0],
        merged[1],
        merged[2],
        merged[3],
        merged[4],
        merged[5],
        merged[6],
        merged[7],
        merged[8],
        merged[9],
        merged[10],
        merged[11],
        small_total[0],
        small_total[1],
        small_total[2],
        small_total[3],
    )


def solution(mesh):
    in_specs = (
        P(None, "dp", "seq", None),
        P(None, "dp", "seq", None),
        P(None, "dp"),
        P(("dp", "seq"), None),
        P(("dp", "seq"), None),
        P(("dp", "seq"), None),
        P(("dp", "seq"), None),
        P(("dp", "seq"), None),
        P(("dp", "seq"), None),
        P(("dp", "seq"), None),
        P(("dp", "seq"), None),
        P(("dp", "seq"), None),
        P(("dp", "seq")),
        P(("dp", "seq")),
        P(("dp", "seq")),
        P(),
        P(),
        P(),
        P(),
    )
    out_specs = (
        P(None, "dp", "seq", None),
        P(None, "dp", "seq", None),
        P(("dp", "seq"), None),
        P(("dp", "seq"), None),
        P(("dp", "seq"), None),
        P(("dp", "seq"), None),
        P(("dp", "seq"), None),
        P(("dp", "seq"), None),
        P(("dp", "seq"), None),
        P(("dp", "seq"), None),
        P(("dp", "seq"), None),
        P(("dp", "seq")),
        P(("dp", "seq")),
        P(("dp", "seq")),
        P(),
        P(),
        P(),
        P(),
    )
    return jax.shard_map(shards, mesh=mesh, in_specs=in_specs, out_specs=out_specs, check_vma=False)
```

profile of v0, /device:TPU:0, one launch (start us, length us, event | category | flops | bytes accessed | tf_op | source)
XLA Modules:
  0.0 2947.8 jit_solution(4157293619148597984)
XLA Ops:
  9.3 70.8 %all-gather.18 = bf16[32,24,16]{1,2,0:T(8,128)(2,1)S(1)} all-gather(bf16[1,24,16]{1,2,0:T(8,128)(2,1)} %bitcast.1217), channel_id=1, replica_groups=mesh['dp'=4,'seq'=8] {'dp','seq'}, dimensions={0}, use_global_device_ids=true | all-gather | bytes 25344 | tf_op jit(solution)/shard_map/all_gather | solution.py:650
  80.7 64.9 %all-gather.17 = bf16[32,24,16]{1,2,0:T(8,128)(2,1)S(1)} all-gather(bf16[1,24,16]{1,2,0:T(8,128)(2,1)} %bitcast.1218), channel_id=1, replica_groups=mesh['dp'=4,'seq'=8] {'dp','seq'}, dimensions={0}, use_global_device_ids=true | all-gather | bytes 25344 | tf_op jit(solution)/shard_map/all_gather | solution.py:649
  146.1 66.4 %all-gather.15 = bf16[32,24,16]{1,2,0:T(8,128)(2,1)S(1)} all-gather(bf16[1,24,16]{1,2,0:T(8,128)(2,1)S(1)} %bitcast.1219), channel_id=1, replica_groups=mesh['dp'=4,'seq'=8] {'dp','seq'}, dimensions={0}, use_global_device_ids=true | all-gather | bytes 25344 | tf_op jit(solution)/shard_map/all_gather | solution.py:647
  213.0 64.0 %all-gather.16 = bf16[32,24,16]{1,2,0:T(8,128)(2,1)S(1)} all-gather(bf16[1,24,16]{1,2,0:T(8,128)(2,1)S(1)} %bitcast.1220), channel_id=1, replica_groups=mesh['dp'=4,'seq'=8] {'dp','seq'}, dimensions={0}, use_global_device_ids=true | all-gather | bytes 25344 | tf_op jit(solution)/shard_map/all_gather | solution.py:648
  320.9 136.4 %while.352 = (s32[]{:T(128)}, f32[2,768,16]{2,0,1:T(2,128)}, f32[2,2,64,768]{3,2,0,1:T(8,128)}, f32[768,16]{1,0:T(8,128)}, f32[2,2,64,768]{2,1,3,0:T(2,128)S(1)}...) while((s32[]{:T(128)}, f32[2,768,16]{2,0,1:T(2,128)}, ...), condition=%wide.region_1.2_spmd.clone.clone.clone, body=%wide.region_0.1_spmd.clone.clone.clone.sunk | while | flops 116588544 | bytes 20349708 | solution.py:111
  321.1 42.1 %fusion.1096 = f32[768,2,64]{2,1,0:T(2,128)S(1)} fusion(f32[64,64,768]{1,0,2:T(8,128)} %get-tuple-element.7761, f32[2,2,64,768]{2,1,3,0:T(2,128)S(1)} %get-tuple-element.7760, s32[]{:T(128)S(6)} %copy.1989), kind=kOutput, calls=%fused_computation.414.clone.1 | convolution fusion | flops 75497472 | bytes 13762564 | tf_op jit(solution)/shard_map/while/body/eval_jaxpr/rsd,...sd->...rd/dot_general | solution.py:84
  389.2 42.1 %fusion.1096 = f32[768,2,64]{2,1,0:T(2,128)S(1)} fusion(f32[64,64,768]{1,0,2:T(8,128)} %get-tuple-element.7761, f32[2,2,64,768]{2,1,3,0:T(2,128)S(1)} %get-tuple-element.7760, s32[]{:T(128)S(6)} %copy.1989), kind=kOutput, calls=%fused_computation.414.clone.1 | convolution fusion | flops 75497472 | bytes 13762564 | tf_op jit(solution)/shard_map/while/body/eval_jaxpr/rsd,...sd->...rd/dot_general | solution.py:84
  460.9 138.1 %while.353 = (s32[]{:T(128)}, f32[2,768,16]{2,0,1:T(2,128)}, f32[2,2,64,768]{3,2,0,1:T(8,128)}, f32[768,16]{1,0:T(8,128)}, f32[2,2,64,768]{2,1,3,0:T(2,128)S(1)}...) while((s32[]{:T(128)}, f32[2,768,16]{2,0,1:T(2,128)}, ...), condition=%wide.region_18.19_spmd.clone.clone.clone, body=%wide.region_17.18_spmd.clone.clone.clone.sunk | while | flops 116588544 | bytes 20349708 | solution.py:111
  461.2 42.8 %fusion.1104 = f32[768,2,64]{2,1,0:T(2,128)} fusion(f32[64,64,768]{1,0,2:T(8,128)} %get-tuple-element.7800, f32[2,2,64,768]{2,1,3,0:T(2,128)S(1)} %get-tuple-element.7799, s32[]{:T(128)S(6)} %copy.1998), kind=kOutput, calls=%fused_computation.443.clone.1 | convolution fusion | flops 75497472 | bytes 13762564 | tf_op jit(solution)/shard_map/while/body/eval_jaxpr/rsd,...sd->...rd/dot_general | solution.py:84
  530.1 42.8 %fusion.1104 = f32[768,2,64]{2,1,0:T(2,128)} fusion(f32[64,64,768]{1,0,2:T(8,128)} %get-tuple-element.7800, f32[2,2,64,768]{2,1,3,0:T(2,128)S(1)} %get-tuple-element.7799, s32[]{:T(128)S(6)} %copy.1998), kind=kOutput, calls=%fused_computation.443.clone.1 | convolution fusion | flops 75497472 | bytes 13762564 | tf_op jit(solution)/shard_map/while/body/eval_jaxpr/rsd,...sd->...rd/dot_general | solution.py:84
  641.0 34.3 %all-gather = f32[16,768,16]{1,2,0:T(8,128)} all-gather(f32[2,768,16]{1,2,0:T(8,128)S(1)} %get-tuple-element.6534), channel_id=2, replica_groups=mesh['dp'=4,'seq'=8] {'seq'}, dimensions={0}, use_global_device_ids=true | all-gather | bytes 884736 | tf_op jit(solution)/shard_map/all_gather | solution.py:19
  685.3 37.0 %all-reduce.12 = (bf16[768]{0:T(1024)(128)(2,1)S(1)}, bf16[768]{0:T(1024)(128)(2,1)S(1)}, bf16[768]{0:T(1024)(128)(2,1)}) all-reduce(bf16[768]{0:T(1024)(128)(2,1)S(1)} %dynamic-update-slice, bf16[768]{0:T(1024)(128)(2,1)S(1)} %dynamic-update-slice.1, bf16[768]{0:T(1024)(128)(2,1)S(1)} %dynamic-update-slice.2), channel_id=1, replica_groups=mesh['dp'=4,'seq'=8] {'dp','seq'}, use_global_device_ids=true, to_apply=%add | all-reduce | flops 2304 | bytes 9216
  745.8 34.4 %all-gather.3 = f32[16,768,16]{1,2,0:T(8,128)} all-gather(f32[2,768,16]{1,2,0:T(8,128)S(1)} %get-tuple-element.6535), channel_id=5, replica_groups=mesh['dp'=4,'seq'=8] {'seq'}, dimensions={0}, use_global_device_ids=true | all-gather | bytes 884736 | tf_op jit(solution)/shard_map/all_gather | solution.py:19
  845.6 32.9 %while.343 = (s32[]{:T(128)}, f32[2,768,16]{2,0,1:T(2,128)}, f32[2,2,768,16]{3,1,2,0:T(2,128)}, f32[1,768,16]{2,1,0:T(8,128)}, f32[2,2,64,768]{2,1,3,0:T(2,128)S...) while((s32[]{:T(128)}, f32[2,768,16]{2,0,1:T(2,128)}, ...), condition=%wide.region_64.65_spmd.clone, body=%wide.region_63.64_spmd.clone.sunk | while | flops 20545540 | bytes 3047808 | solution.py:111
  880.2 32.9 %while.341 = (s32[]{:T(128)}, f32[2,768,16]{2,0,1:T(2,128)}, f32[2,2,768,16]{3,1,2,0:T(2,128)}, f32[1,768,16]{2,1,0:T(8,128)}, f32[2,2,64,768]{2,1,3,0:T(2,128)S...) while((s32[]{:T(128)}, f32[2,768,16]{2,0,1:T(2,128)}, ...), condition=%wide.region_47.48_spmd.clone, body=%wide.region_46.47_spmd.clone.sunk | while | flops 20545540 | bytes 3047808 | solution.py:111
  930.5 33.2 %all-gather.10 = bf16[1,1024,128]{2,1,0:T(8,128)(2,1)} all-gather(bf16[1,128,128]{2,1,0:T(8,128)(2,1)S(1)} %constant_dynamic-slice_fusion.11), channel_id=12, replica_groups=mesh['dp'=4,'seq'=8] {'seq'}, dimensions={1}, use_global_device_ids=true | all-gather | bytes 294912 | tf_op jit(solution)/shard_map/all_gather | solution.py:515
  963.7 33.0 %all-gather.5 = bf16[1,1024,128]{2,1,0:T(8,128)(2,1)} all-gather(bf16[1,128,128]{2,1,0:T(8,128)(2,1)S(1)} %constant_dynamic-slice_fusion.14), channel_id=7, replica_groups=mesh['dp'=4,'seq'=8] {'seq'}, dimensions={1}, use_global_device_ids=true | all-gather | bytes 294912 | tf_op jit(solution)/shard_map/all_gather | solution.py:515
  1069.7 55.6 %all-gather.37.cloned.1.call-done = bf16[1536,768]{1,0:T(8,128)(2,1)} async-done(((bf16[48,768]{1,0:T(8,128)(2,1)}), bf16[1536,768]{1,0:T(8,128)(2,1)}) %all-gather.37.cloned.1.call-update) | async-done | bytes 2359312 | tf_op jit(solution)/shard_map/all_gather | solution.py:646
  1185.2 47.2 %all-gather.11 = f32[1,1024]{1,0:T(1,128)S(1)} all-gather(f32[1,128]{1,0:T(1,128)S(1)} %bitcast.1223), channel_id=13, replica_groups=mesh['dp'=4,'seq'=8] {'seq'}, dimensions={1}, use_global_device_ids=true | all-gather | bytes 4608 | tf_op jit(solution)/shard_map/all_gather | solution.py:519
  1368.5 234.8 %while.355 = (s32[]{:T(128)}, f32[64,64,768]{1,0,2:T(8,128)}, f32[64,768,16]{0,2,1:T(8,128)}, f32[768,16]{1,0:T(8,128)S(1)}, f32[64,768,16]{0,2,1:T(8,128)}, /*i...) while((s32[]{:T(128)}, f32[64,64,768]{1,0,2:T(8,128)}, ...), condition=%wide.region_67.68_spmd.clone.clone.clone, body=%wide.region_65.67_spmd.clone.clone.clone.sunk | while | flops 239284224 | bytes 187863472 | solution.py:111
  1368.7 42.4 %bitcast_add_fusion.30 = f32[64,64,768]{1,0,2:T(8,128)} fusion(f32[64,64,768]{1,0,2:T(8,128)} %get-tuple-element.8197, pred[]{:T(512)S(6)} %compare.275, f32[2,2,64,768]{2,1,3,0:T(2,128)S(1)} %get-tuple-element.8223, s32[]{:T(128)S(6)} %sub.2211, f32[2,2,64,768]{2,1,3,0:T(2,128)S(1)} %get-tuple-element.8222), kind=kOutput, calls=%fused_computation.501.clone.1 | convolution fusion | flops 81788928 | bytes 26740224 | tf_op jit(solution)/shard_map/transpose(jvp())/while/body/eval_jaxpr/rsd,...sd->...rd/dot_general | solution.py:84
  1483.8 44.7 %bitcast_add_fusion.30 = f32[64,64,768]{1,0,2:T(8,128)} fusion(f32[64,64,768]{1,0,2:T(8,128)} %get-tuple-element.8197, pred[]{:T(512)S(6)} %compare.275, f32[2,2,64,768]{2,1,3,0:T(2,128)S(1)} %get-tuple-element.8223, s32[]{:T(128)S(6)} %sub.2211, f32[2,2,64,768]{2,1,3,0:T(2,128)S(1)} %get-tuple-element.8222), kind=kOutput, calls=%fused_computation.501.clone.1 | convolution fusion | flops 81788928 | bytes 26740224 | tf_op jit(solution)/shard_map/transpose(jvp())/while/body/eval_jaxpr/rsd,...sd->...rd/dot_general | solution.py:84
  1653.9 42.0 %all-gather.8 = f32[1,1024]{1,0:T(1,128)S(1)} all-gather(f32[1,128]{1,0:T(1,128)S(1)} %bitcast.1214), channel_id=10, replica_groups=mesh['dp'=4,'seq'=8] {'seq'}, dimensions={1}, use_global_device_ids=true | all-gather | bytes 4608 | tf_op jit(solution)/shard_map/all_gather | solution.py:520
  1832.4 260.7 %while.354 = (s32[]{:T(128)}, f32[64,64,768]{1,0,2:T(8,128)}, f32[64,768,16]{0,2,1:T(8,128)}, f32[768,16]{1,0:T(8,128)S(1)}, f32[64,768,16]{0,2,1:T(8,128)}, /*i...) while((s32[]{:T(128)}, f32[64,64,768]{1,0,2:T(8,128)}, ...), condition=%wide.region_50.51_spmd.clone.clone.clone, body=%wide.region_48.50_spmd.clone.clone.clone.sunk | while | flops 239284224 | bytes 187863472 | solution.py:111
  1853.1 42.4 %bitcast_add_fusion.27 = f32[64,64,768]{1,0,2:T(8,128)} fusion(f32[64,64,768]{1,0,2:T(8,128)} %get-tuple-element.8407, pred[]{:T(512)S(6)} %compare.274, f32[2,2,64,768]{2,1,3,0:T(2,128)S(1)} %get-tuple-element.8433, s32[]{:T(128)S(6)} %sub.2210, f32[2,2,64,768]{2,1,3,0:T(2,128)S(1)} %get-tuple-element.8432), kind=kOutput, calls=%fused_computation.454.clone.1 | convolution fusion | flops 81788928 | bytes 26740224 | tf_op jit(solution)/shard_map/transpose(jvp())/while/body/eval_jaxpr/rsd,...sd->...rd/dot_general | solution.py:84
  1968.2 44.7 %bitcast_add_fusion.27 = f32[64,64,768]{1,0,2:T(8,128)} fusion(f32[64,64,768]{1,0,2:T(8,128)} %get-tuple-element.8407, pred[]{:T(512)S(6)} %compare.274, f32[2,2,64,768]{2,1,3,0:T(2,128)S(1)} %get-tuple-element.8433, s32[]{:T(128)S(6)} %sub.2210, f32[2,2,64,768]{2,1,3,0:T(2,128)S(1)} %get-tuple-element.8432), kind=kOutput, calls=%fused_computation.454.clone.1 | convolution fusion | flops 81788928 | bytes 26740224 | tf_op jit(solution)/shard_map/transpose(jvp())/while/body/eval_jaxpr/rsd,...sd->...rd/dot_general | solution.py:84
  2264.8 75.3 %all-reduce.15.cloned.1.call-done = (f32[768,16]{0,1:T(8,128)}, f32[768,16]{0,1:T(8,128)}, f32[768,16]{0,1:T(8,128)}, f32[768,16]{0,1:T(8,128)}, f32[768]{0:T(10...) async-done(((f32[768,16]{0,1:T(8,128)}, f32[768,16]{0,1:T(8,128)}, f32[768,16]{0,1:T(8,128)}, ...) | async-done | bytes 207504
  2349.4 105.6 %reduce-scatter.16.cloned.1.call-done = f32[24,1536]{1,0:T(8,128)} async-done(((f32[768,1536]{1,0:T(8,128)}), f32[24,1536]{1,0:T(8,128)}) %reduce-scatter.16.cloned.1.call-update) | async-done | bytes 147472 | tf_op jit(solution)/shard_map/reduce_scatter | solution.py:703
  2455.0 112.0 %reduce-scatter.18.cloned.1.call-done = f32[48,768]{1,0:T(8,128)} async-done(((f32[1536,768]{1,0:T(8,128)}), f32[48,768]{1,0:T(8,128)}) %reduce-scatter.18.cloned.1.call-update) | async-done | bytes 147472 | tf_op jit(solution)/shard_map/reduce_scatter | solution.py:704
  2567.0 113.1 %reduce-scatter.14.cloned.1.call-done = f32[48,768]{1,0:T(8,128)} async-done(((f32[1536,768]{1,0:T(8,128)}), f32[48,768]{1,0:T(8,128)}) %reduce-scatter.14.cloned.1.call-update) | async-done | bytes 147472 | tf_op jit(solution)/shard_map/reduce_scatter | solution.py:702
  2680.1 112.0 %reduce-scatter.20.cloned.1.call-done = f32[24,1536]{1,0:T(8,128)} async-done(((f32[768,1536]{1,0:T(8,128)}), f32[24,1536]{1,0:T(8,128)}) %reduce-scatter.20.cloned.1.call-update) | async-done | bytes 147472
  2792.1 144.0 %reduce-scatter.22.cloned.1.call-done = f32[24,3200]{1,0:T(8,128)} async-done(((f32[768,3200]{1,0:T(8,128)}), f32[24,3200]{1,0:T(8,128)}) %reduce-scatter.22.cloned.1.call-update) | async-done | bytes 307216
  (1348 shorter events, 1479.0 us)
Async XLA Ops:
  7.2 138.9 %copy-start.274 = (bf16[24,16]{0,1:T(8,128)(2,1)S(1)}, bf16[24,16]{0,1:T(8,128)(2,1)}, u32[]{:S(2)}) copy-start(bf16[24,16]{0,1:T(8,128)(2,1)} %param.73) | copy-start | bytes 2308
  7.2 205.8 %copy-start.275 = (bf16[24,16]{0,1:T(8,128)(2,1)S(1)}, bf16[24,16]{0,1:T(8,128)(2,1)}, u32[]{:S(2)}) copy-start(bf16[24,16]{0,1:T(8,128)(2,1)} %param.74) | copy-start | bytes 2308
  7.2 799.1 %all-gather.31.cloned.1.call-start = ((), (), s32[]{:S(2)}) async-start(), calls=%async_computation.6 | async-start | bytes 2433024 | tf_op jit(solution)/shard_map/all_gather | solution.py:642
  7.9 802.4 %all-gather.29.cloned.1.call-start = ((), (), s32[]{:S(2)}) async-start(), calls=%async_computation.5 | async-start | bytes 5068800 | tf_op jit(solution)/shard_map/all_gather | solution.py:643
  8.7 988.6 %all-gather.39.cloned.1.call-start = ((), (), s32[]{:S(2)}) async-start(), calls=%async_computation.10 | async-start | bytes 3833856 | tf_op jit(solution)/shard_map/all_gather | solution.py:372
  8.8 278.9 %copy-start.179 = (f32[64,64]{1,0:T(8,128)}, f32[64,64]{1,0:T(8,128)S(1)}, u32[]{:S(2)}) copy-start(f32[64,64]{1,0:T(8,128)S(1)} %iota_subtract_fusion) | copy-start | bytes 49156
  80.7 198.5 %copy-start.140 = (f32[768,16]{0,1:T(8,128)}, f32[768,16]{0,1:T(8,128)S(1)}, u32[]{:S(2)}) copy-start(f32[768,16]{0,1:T(8,128)S(1)} %reshape.1529) | copy-start | bytes 147460
  145.9 134.9 %copy-start.169 = (bf16[2,2,128,768]{3,2,1,0:T(8,128)(2,1)S(1)}, bf16[2,2,128,768]{3,2,1,0:T(8,128)(2,1)}, u32[]{:S(2)}) copy-start(bf16[2,2,128,768]{3,2,1,0:T(8,128)(2,1)} %param.65) | copy-start | bytes 2359300
  146.1 135.9 %copy-start.184 = (f32[768,16]{0,1:T(8,128)}, f32[768,16]{0,1:T(8,128)S(1)}, u32[]{:S(2)}) copy-start(f32[768,16]{0,1:T(8,128)S(1)} %reshape.1524) | copy-start | bytes 147460
  818.2 204.6 %all-gather.41.cloned.1.call-start = ((), (), s32[]{:S(2)}) async-start(), calls=%async_computation.11 | async-start | bytes 3833856 | tf_op jit(solution)/shard_map/all_gather | solution.py:372
  825.8 228.1 %all-gather.33.cloned.1.call-start = ((), (), s32[]{:S(2)}) async-start(), calls=%async_computation.7 | async-start | bytes 2433024 | tf_op jit(solution)/shard_map/all_gather | solution.py:644
  826.4 239.6 %all-gather.35.cloned.1.call-start = ((), (), s32[]{:S(2)}) async-start(), calls=%async_computation.8 | async-start | bytes 2433024 | tf_op jit(solution)/shard_map/all_gather | solution.py:645
  827.0 298.3 %all-gather.37.cloned.1.call-start = ((), (), s32[]{:S(2)}) async-start(), calls=%async_computation.9 | async-start | bytes 2433024 | tf_op jit(solution)/shard_map/all_gather | solution.py:646
  827.7 446.9 %all-gather.45.cloned.1.call-start = ((), (), s32[]{:S(2)}) async-start(), calls=%async_computation.13 | async-start | bytes 3538944 | tf_op jit(solution)/shard_map/all_gather | solution.py:516
  833.0 225.5 %copy-start.224 = (s32[128]{0:T(128)}, s32[128]{0:T(128)S(1)}, u32[]{:S(2)}) copy-start(s32[128]{0:T(128)S(1)} %iota_add_fusion.24) | copy-start | bytes 1540
  843.0 426.2 %copy-start.149 = (f32[768]{0:T(1024)}, f32[768]{0:T(1024)S(1)}, u32[]{:S(2)}) copy-start(f32[768]{0:T(1024)S(1)} %convert_element_type.308) | copy-start | bytes 9220
  1064.0 205.3 %copy-start.20 = (f32[256,768]{1,0:T(8,128)}, f32[256,768]{1,0:T(8,128)S(1)}, u32[]{:S(2)}) copy-start(f32[256,768]{1,0:T(8,128)S(1)} %get-tuple-element.6443) | copy-start | bytes 2359300
  1064.0 205.3 %copy-start.216 = (f32[256]{0:T(256)}, f32[256]{0:T(256)S(1)}, u32[]{:S(2)}) copy-start(f32[256]{0:T(256)S(1)} %broadcast_multiply_fusion.8) | copy-start | bytes 3076
  1145.2 591.0 %all-gather.43.cloned.1.call-start = ((), (), s32[]{:S(2)}) async-start(), calls=%async_computation.12 | async-start | bytes 3538944 | tf_op jit(solution)/shard_map/all_gather | solution.py:516
  1174.7 93.2 %copy-start.111 = (bf16[256,1536]{1,0:T(8,128)(2,1)S(1)}, bf16[256,1536]{1,0:T(8,128)(2,1)}, u32[]{:S(2)}) copy-start(bf16[256,1536]{1,0:T(8,128)(2,1)} %copy-done.110) | copy-start | bytes 2359300
  1174.7 93.2 %copy-start.178 = (f32[128,128]{0,1:T(8,128)S(1)}, f32[128,128]{0,1:T(8,128)}, u32[]{:S(2)}) copy-start(f32[128,128]{0,1:T(8,128)} %copy-done.176) | copy-start | bytes 196612
  1174.7 93.2 %copy-start.225 = (s32[128]{0:T(128)S(1)}, s32[128]{0:T(128)}, u32[]{:S(2)}) copy-start(s32[128]{0:T(128)} %copy-done.224) | copy-start | bytes 1540
  1174.7 93.2 %copy-start.247 = (s32[128]{0:T(128)S(1)}, s32[128]{0:T(128)}, u32[]{:S(2)}) copy-start(s32[128]{0:T(128)} %copy-done.245) | copy-start | bytes 1540
  1174.7 93.2 %copy-start.288 = (f32[128]{0:T(128)S(1)}, f32[128]{0:T(128)}, u32[]{:S(2)}) copy-start(f32[128]{0:T(128)} %get-tuple-element.6551) | copy-start | bytes 1540
  1174.8 94.5 %copy-start.88 = (bf16[256,1536]{1,0:T(8,128)(2,1)S(1)}, bf16[256,1536]{1,0:T(8,128)(2,1)}, u32[]{:S(2)}) copy-start(bf16[256,1536]{1,0:T(8,128)(2,1)} %copy-done.87) | copy-start | bytes 2359300
  1174.8 94.5 %copy-start.222 = (f32[256]{0:T(256)S(1)}, f32[256]{0:T(256)}, u32[]{:S(2)}) copy-start(f32[256]{0:T(256)} %copy-done.221) | copy-start | bytes 3076
  1617.6 722.5 %all-reduce.15.cloned.1.call-start = ((), (), s32[]{:S(2)}) async-start(), calls=%async_computation.19 | async-start | bytes 421888
  2214.7 240.3 %reduce-scatter.16.cloned.1.call-start = ((), (), s32[]{:S(2)}) async-start(), calls=%async_computation.15 | async-start | bytes 4866048 | tf_op jit(solution)/shard_map/reduce_scatter | solution.py:703
  2220.4 346.6 %reduce-scatter.18.cloned.1.call-start = ((), (), s32[]{:S(2)}) async-start(), calls=%async_computation.16 | async-start | bytes 4866048 | tf_op jit(solution)/shard_map/reduce_scatter | solution.py:704
  2227.4 452.7 %reduce-scatter.14.cloned.1.call-start = ((), (), s32[]{:S(2)}) async-start(), calls=%async_computation.14 | async-start | bytes 4866048 | tf_op jit(solution)/shard_map/reduce_scatter | solution.py:702
  2232.5 559.6 %reduce-scatter.20.cloned.1.call-start = ((), (), s32[]{:S(2)}) async-start(), calls=%async_computation.17 | async-start | bytes 4866048
  2248.5 687.7 %reduce-scatter.22.cloned.1.call-start = ((), (), s32[]{:S(2)}) async-start(), calls=%async_computation.18 | async-start | bytes 10137600
  (367 other events, 6146.5 us)
Sparse Core Ops, SparseCore 0:
  11.0 60.4 all-gather.30
  74.4 63.8 all-gather.28
  818.3 63.3 all-gather.38
  883.7 64.5 all-gather.40
  951.2 55.4 all-gather.32
  1009.5 56.5 all-gather.34
  1069.0 56.2 all-gather.36
  1145.3 59.3 all-gather.44
  1617.7 56.8 all-gather.42
  2214.8 125.2 all-reduce.14
  2347.0 107.9 reduce-scatter.15
  2460.9 106.0 reduce-scatter.17
  2574.0 106.0 reduce-scatter.13
  2686.0 106.0 reduce-scatter.19
  2799.5 136.5 reduce-scatter.21
where the time goes:
time: 2960 us; the launch traced here: 2950 us
  matrix products  1150 us (39%)
  waiting for transfers between devices  723 us (24%)
  blocking collectives  657 us (22%)
  local copies, waits for them, and re-layouts  205 us (7%)
  other arithmetic  150 us (5%)
  loops' own time  33.1 us (1%)
    dot_general x12, matrix products, ema_step(): jnp.einsum('rsd,...sd->...rd', toeplitz, block_input, precision=highest)  434 us
    unnamed x18, waiting for transfers between devices  335 us
    dot_general x16, matrix products, ema_step(): jnp.einsum('rdh,...rd->...dh', inject, block_input, precision=highest)  200 us
    all_gather x5, blocking collectives, carried_in(): pieces = jax.tree.map(lambda part: lax.all_gather(part, axis), value)  164 us
    dot_general x12, matrix products, ema_step(): jnp.einsum('rdh,...dh->...rd', powers, ema_state, precision=highest)  148 us
    reduce_scatter x1, waiting for transfers between devices, shards(): lax.psum_scatter(full_grads[2], ('dp', 'seq'), scatter_dimension=0, tiled...  113 us
    reduce_scatter x1, waiting for transfers between devices, shards(): lax.psum_scatter(full_grads[4], ('dp', 'seq'), scatter_dimension=0, tiled...  112 us
    reduce_scatter x1, waiting for transfers between devices, shards(): lax.psum_scatter(full_grads[3], ('dp', 'seq'), scatter_dimension=0, tiled...  106 us
  transfers between devices with their start and end apart: 15, of which 8 were waited for; matrix products, arithmetic and copies ran while one was open for 25% of the time, Pallas kernels for 0%

commit v1 on v0

v1 whole, which is shorter than its diff:
```python
import functools

import jax
import jax.numpy as jnp
import numpy as np
from jax import lax
from jax.experimental import pallas as pl
from jax.experimental.pallas import tpu as pltpu
from jax.sharding import PartitionSpec as P

epsilon = 1e-05
masked_fill = -1e30
MESH = pl.DeviceIdType.MESH
ANY = pl.BlockSpec(memory_space=pl.ANY)
VM = pl.BlockSpec(memory_space=pltpu.VMEM)
SM = pl.BlockSpec(memory_space=pltpu.SMEM)
F32 = jnp.float32
BF16 = jnp.bfloat16
SEG = 8
LANES = 128


def bucket_edges(bucket_count):
    edge_list = [0]
    middle = bucket_count // 2
    for number in range(1, bucket_count):
        edge_list.append(number if number < middle else int(middle * 2 ** ((number - middle) / 2)))
    return edge_list


class Layout:
    def __init__(self, dp, seq, micro, items):
        self.dp, self.S = dp, seq
        self.C = 2
        self.Y = dp // 2
        self.X = min(self.Y, seq)
        self.Z = seq // self.X
        self.items = items
        self.MS = micro * items
        self.Q = 2 * self.MS
        self.Cq = seq // self.Q
        self.G = 2 * self.Cq
        self.BL = seq // self.G

    def here(self):
        d, b = lax.axis_index("dp"), lax.axis_index("seq")
        return d // 2, d % 2, b // self.X, b % self.X, b


class Wire:
    def __init__(self, lay, send, recv):
        self.lay, self.send, self.recv, self.count = lay, send, recv, 0
        self.sent = []

    def to(self, y, c, z, x):
        return (y * 2 + c, z * self.lay.X + x)

    def start(self, src, dst, target):
        number = self.count
        self.count += 1
        copy = pltpu.make_async_remote_copy(
            src_ref=src,
            dst_ref=dst,
            send_sem=self.send.at[number],
            recv_sem=self.recv.at[number],
            device_id=target,
            device_id_type=MESH,
        )
        copy.start()
        self.sent.append(copy)
        return copy

    def finish(self):
        for copy in self.sent:
            copy.wait_send()


def greet(lay):
    y, c, z, x, b = lay.here()
    barrier = pltpu.get_barrier_semaphore()
    plane = 2 * lay.S

    def one(k, carry):
        other = (c * lay.S + b + k) % plane
        pl.semaphore_signal(
            barrier, inc=1, device_id=(y * 2 + other // lay.S, other % lay.S), device_id_type=MESH
        )
        return carry

    lax.fori_loop(1, plane, one, 0)
    for k in range(1, lay.Y):
        pl.semaphore_signal(
            barrier, inc=1, device_id=(((y + k) % lay.Y) * 2 + c, b), device_id_type=MESH
        )
    pl.semaphore_wait(barrier, plane - 1 + lay.Y - 1)


def half_columns(columns):
    return ((columns // LANES + 1) // 2) * LANES


def reshard_in(lay, sources, targets, send, recv, local):
    y, c, z, x, b = lay.here()
    g = b // lay.BL
    slot = b % lay.BL
    qm = b // lay.Cq
    gm = (b % lay.Cq) * 2 + c

    def begin():
        for n, (source, target) in enumerate(zip(sources, targets)):
            for ms in range(lay.MS):
                seq_to = (ms * 2 + c) * lay.Cq + g // 2
                mine = jnp.logical_and(seq_to == b, g % 2 == c)
                block = source.at[ms // lay.items, ms % lay.items]

                @pl.when(jnp.logical_not(mine))
                def _():
                    pltpu.make_async_remote_copy(
                        src_ref=block,
                        dst_ref=target.at[slot],
                        send_sem=send.at[n, ms],
                        recv_sem=recv.at[n, slot],
                        device_id=(y * 2 + g % 2, seq_to),
                        device_id_type=MESH,
                    ).start()

                @pl.when(mine)
                def _():
                    pltpu.make_async_copy(block, target.at[slot], local.at[n]).start()

    def wait(n):
        source, target = sources[n], targets[n]
        for ms in range(lay.MS):
            seq_to = (ms * 2 + c) * lay.Cq + g // 2
            mine = jnp.logical_and(seq_to == b, g % 2 == c)
            block = source.at[ms // lay.items, ms % lay.items]

            @pl.when(jnp.logical_not(mine))
            def _():
                pltpu.make_async_remote_copy(
                    src_ref=block,
                    dst_ref=target.at[slot],
                    send_sem=send.at[n, ms],
                    recv_sem=recv.at[n, slot],
                    device_id=(y * 2 + g % 2, seq_to),
                    device_id_type=MESH,
                ).wait_send()

            @pl.when(mine)
            def _():
                pltpu.make_async_copy(block, target.at[slot], local.at[n]).wait()

        for j in range(lay.BL):
            from_b = gm * lay.BL + j
            own = jnp.logical_and(from_b == b, qm % 2 == c)

            @pl.when(jnp.logical_not(own))
            def _():
                pltpu.make_async_remote_copy(
                    src_ref=source.at[0, 0],
                    dst_ref=target.at[j],
                    send_sem=send.at[n, 0],
                    recv_sem=recv.at[n, j],
                    device_id=(y * 2 + qm % 2, from_b),
                    device_id_type=MESH,
                ).wait_recv()

    return begin, wait


def reshard_out(lay, sources, targets, send, recv, local):
    y, c, z, x, b = lay.here()
    g = b // lay.BL
    qm = b // lay.Cq
    gm = (b % lay.Cq) * 2 + c
    ms_to = qm // 2
    m_to, s_to = ms_to // lay.items, ms_to % lay.items

    def copies(n, j):
        from_b = gm * lay.BL + j
        own = jnp.logical_and(from_b == b, qm % 2 == c)
        remote = pltpu.make_async_remote_copy(
            src_ref=sources[n].at[j],
            dst_ref=targets[n].at[m_to, s_to],
            send_sem=send.at[n, j],
            recv_sem=recv.at[n, ms_to],
            device_id=(y * 2 + qm % 2, from_b),
            device_id_type=MESH,
        )
        near = pltpu.make_async_copy(sources[n].at[j], targets[n].at[m_to, s_to], local.at[n])
        return own, remote, near

    def begin(n):
        for j in range(lay.BL):
            own, remote, near = copies(n, j)
            pl.when(jnp.logical_not(own))(remote.start)
            pl.when(own)(near.start)

    def wait(n):
        for j in range(lay.BL):
            own, remote, near = copies(n, j)
            pl.when(jnp.logical_not(own))(remote.wait_send)
            pl.when(own)(near.wait)
        for ms in range(lay.MS):
            seq_at = (ms * 2 + c) * lay.Cq + g // 2
            own = jnp.logical_and(seq_at == b, g % 2 == c)

            @pl.when(jnp.logical_not(own))
            def _():
                pltpu.make_async_remote_copy(
                    src_ref=sources[n].at[0],
                    dst_ref=targets[n].at[ms // lay.items, ms % lay.items],
                    send_sem=send.at[n, 0],
                    recv_sem=recv.at[n, ms],
                    device_id=(y * 2 + g % 2, seq_at),
                    device_id_type=MESH,
                ).wait_recv()

    return begin, wait


def gather_kernel(lay, count, refs):
    tok, cot = refs[0], refs[1]
    shards = refs[2 : 2 + count]
    tok_out, cot_out = refs[2 + count], refs[3 + count]
    fulls = refs[4 + count : 4 + 2 * count]
    send, recv, local, t_send, t_recv, t_local = refs[4 + 2 * count :]
    y, c, z, x, b = lay.here()
    X, Y, Z = lay.X, lay.Y, lay.Z
    greet(lay)
    wire = Wire(lay, send, recv)
    begin, wait = reshard_in(lay, (tok, cot), (tok_out, cot_out), t_send, t_recv, t_local)

    def own(n):
        copy = pltpu.make_async_copy(shards[n], fulls[n].at[y, c, z, x], local.at[n])
        copy.start()
        return copy

    owns = [own(n) for n in range(count)]
    arrived = [dict() for n in range(count)]

    def stage_z(n):
        arrived[n]["z"] = [
            wire.start(shards[n], fulls[n].at[y, c, z, x], wire.to(y, c, (z + k) % Z, x))
            for k in range(1, Z)
        ]

    def parts(n):
        columns = shards[n].shape[1]
        left = half_columns(columns)
        result = [(0, left)]
        if left < columns:
            result.append((left, columns - left))
        return result

    def to_core(n, block):
        arrived[n].setdefault("core", []).append(wire.start(block, block, wire.to(y, 1 - c, z, x)))

    def stage_one(n):
        owns[n].wait()
        for copy in arrived[n]["z"]:
            copy.wait_recv()
        full = fulls[n]
        for half, (at, width) in enumerate(parts(n)):
            block = full.at[y, c, :, x, :, pl.ds(at, width)]
            if half == 0:
                arrived[n]["x0"] = [
                    wire.start(block, block, wire.to(y, c, z, (x + k) % X)) for k in range(1, X)
                ]
            else:
                arrived[n]["y1"] = [
                    wire.start(block, block, wire.to((y + k) % Y, c, z, x)) for k in range(1, Y)
                ]
        to_core(n, full.at[y, c, :, x])

    def stage_two(n):
        full = fulls[n]
        for half, (at, width) in enumerate(parts(n)):
            cols = pl.ds(at, width)
            if half == 0:
                for copy in arrived[n]["x0"]:
                    copy.wait_recv()
                block = full.at[y, c, :, :, :, cols]
                arrived[n]["y0"] = [
                    wire.start(block, block, wire.to((y + k) % Y, c, z, x)) for k in range(1, Y)
                ]
                for k in range(1, X):
                    to_core(n, full.at[y, c, :, (x + X - k) % X, :, cols])
            else:
                for copy in arrived[n]["y1"]:
                    copy.wait_recv()
                block = full.at[:, c, :, x, :, cols]
                arrived[n]["x1"] = [
                    wire.start(block, block, wire.to(y, c, z, (x + k) % X)) for k in range(1, X)
                ]
                for k in range(1, Y):
                    to_core(n, full.at[(y + Y - k) % Y, c, :, x, :, cols])

    def stage_three(n):
        full = fulls[n]
        for half, (at, width) in enumerate(parts(n)):
            cols = pl.ds(at, width)
            if half == 0:
                for k, copy in enumerate(arrived[n]["y0"], 1):
                    copy.wait_recv()
                    to_core(n, full.at[(y + Y - k) % Y, c, :, :, :, cols])
            else:
                for k, copy in enumerate(arrived[n]["x1"], 1):
                    copy.wait_recv()
                    to_core(n, full.at[:, c, :, (x + X - k) % X, :, cols])

    stage_z(0)
    begin()
    for n in range(1, count):
        stage_z(n)
    for turn in range(count + 2):
        if turn < count:
            stage_one(turn)
        if 0 <= turn - 1 < count:
            stage_two(turn - 1)
        if 0 <= turn - 2:
            stage_three(turn - 2)
    for n in range(count):
        for copy in arrived[n]["core"]:
            copy.wait_recv()
    wait(0)
    wait(1)
    wire.finish()


def gather_all(lay, tokens, cotangent, shards):
    count = len(shards)
    micro, items, rows, width = tokens.shape
    per = (lay.Z - 1) + 2 * (lay.X - 1 + lay.Y - 1) + 1 + 2 * (lay.X - 1 + lay.Y - 1)
    blocks = jax.ShapeDtypeStruct((lay.BL, rows, width), BF16)
    outs = [blocks, blocks] + [
        jax.ShapeDtypeStruct((lay.Y, 2, lay.Z, lay.X) + shard.shape, shard.dtype)
        for shard in shards
    ]

    def body(*refs):
        gather_kernel(lay, count, refs)

    result = pl.pallas_call(
        body,
        out_shape=outs,
        in_specs=[ANY] * (2 + count),
        out_specs=[ANY] * (2 + count),
        scratch_shapes=[
            pltpu.SemaphoreType.DMA((count * per,)),
            pltpu.SemaphoreType.DMA((count * per,)),
            pltpu.SemaphoreType.DMA((count,)),
            pltpu.SemaphoreType.DMA((2, lay.MS)),
            pltpu.SemaphoreType.DMA((2, lay.BL)),
            pltpu.SemaphoreType.DMA((2,)),
        ],
        compiler_params=pltpu.CompilerParams(
            collective_id=0, has_side_effects=True, vmem_limit_bytes=16 * 2**20
        ),
        name="gather_all",
    )(tokens, cotangent, *shards)
    return result[0], result[1], result[2:]


def add_blocks(total, index, extra, extra_index, counts, width_at):
    size = int(np.prod(counts)) if counts else 1

    def one(i, carry):
        places = []
        for extent in reversed(counts):
            places.insert(0, i % extent)
            i = i // extent
        a, e = index(*places), extra_index(*places)
        summed = total[a].astype(F32) + extra[e].astype(F32)
        total[a] = summed.astype(total.dtype)
        return carry

    lax.fori_loop(0, size, one, 0)


def scatter_kernel(lay, count, out_count, refs):
    grads = refs[:count]
    small = refs[count]
    outs_in = refs[count + 1 : count + 1 + out_count]
    at = count + 1 + out_count
    results = refs[at : at + count]
    small_out = refs[at + count]
    outs_to = refs[at + count + 1 : at + count + 1 + out_count]
    at = at + count + 1 + out_count
    bufs = refs[at : at + 7 * count]
    at += 7 * count
    small_acc, small_recv = refs[at], refs[at + 1]
    send, recv, local, t_send, t_recv, t_local = refs[at + 2 :]
    y, c, z, x, b = lay.here()
    X, Y, Z = lay.X, lay.Y, lay.Z
    greet(lay)
    wire = Wire(lay, send, recv)
    begin, wait = reshard_out(lay, outs_in, outs_to, t_send, t_recv, t_local)
    arrived = [dict() for n in range(count)]

    def buf(n, name):
        return bufs[7 * n + ("acc", "core", "x0", "y1", "y0", "x1", "z").index(name)]

    def parts(n):
        columns = grads[n].shape[-1]
        left = half_columns(columns)
        result = [(0, left)]
        if left < columns:
            result.append((left, columns - left))
        return result

    def stage_core(n):
        arrived[n]["core"] = [
            wire.start(grads[n].at[:, 1 - c], buf(n, "core"), wire.to(y, 1 - c, z, x))
        ]
        copy = pltpu.make_async_copy(grads[n].at[:, c], buf(n, "acc"), local.at[n])
        copy.start()
        arrived[n]["own"] = copy

    def stage_one(n):
        arrived[n]["own"].wait()
        arrived[n]["core"][0].wait_recv()
        acc = buf(n, "acc")
        add_blocks(acc, lambda i, j, k: (i, j, k), buf(n, "core"), lambda i, j, k: (i, j, k), (Y, Z, X), None)
        for half, (at, width) in enumerate(parts(n)):
            cols = pl.ds(at, width)
            if half == 0:
                arrived[n]["x0"] = [
                    wire.start(
                        acc.at[:, :, (x + k) % X, :, cols],
                        buf(n, "x0").at[k - 1],
                        wire.to(y, c, z, (x + k) % X),
                    )
                    for k in range(1, X)
                ]
            else:
                arrived[n]["y1"] = [
                    wire.start(
                        acc.at[(y + k) % Y, :, :, :, cols],
                        buf(n, "y1").at[k - 1],
                        wire.to((y + k) % Y, c, z, x),
                    )
                    for k in range(1, Y)
                ]

    def stage_two(n):
        acc = buf(n, "acc")
        for half, (at, width) in enumerate(parts(n)):
            cols = slice(at, at + width)
            view = pl.ds(at, width)
            if half == 0:
                for k, copy in enumerate(arrived[n]["x0"]):
                    copy.wait_recv()
                    add_blocks(
                        acc,
                        lambda i, j: (i, j, x, slice(None), cols),
                        buf(n, "x0"),
                        lambda i, j: (k, i, j),
                        (Y, Z),
                        None,
                    )
                arrived[n]["y0"] = [
                    wire.start(
                        acc.at[(y + k) % Y, :, x, :, view],
                        buf(n, "y0").at[k - 1],
                        wire.to((y + k) % Y, c, z, x),
                    )
                    for k in range(1, Y)
                ]
            else:
                for k, copy in enumerate(arrived[n]["y1"]):
                    copy.wait_recv()
                    add_blocks(
                        acc,
                        lambda i, j: (y, i, j, slice(None), cols),
                        buf(n, "y1"),
                        lambda i, j: (k, i, j),
                        (Z, X),
                        None,
                    )
                arrived[n]["x1"] = [
                    wire.start(
                        acc.at[y, :, (x + k) % X, :, view],
                        buf(n, "x1").at[k - 1],
                        wire.to(y, c, z, (x + k) % X),
                    )
                    for k in range(1, X)
                ]

    def stage_three(n):
        acc = buf(n, "acc")
        for half, (at, width) in enumerate(parts(n)):
            cols = slice(at, at + width)
            name = "y0" if half == 0 else "x1"
            for k, copy in enumerate(arrived[n][name]):
                copy.wait_recv()
                add_blocks(
                    acc,
                    lambda i: (y, i, x, slice(None), cols),
                    buf(n, name),
                    lambda i: (k, i),
                    (Z,),
                    None,
                )
        arrived[n]["z"] = [
            wire.start(
                acc.at[y, (z + k) % Z, x], buf(n, "z").at[k - 1], wire.to(y, c, (z + k) % Z, x)
            )
            for k in range(1, Z)
        ]

    def stage_four(n):
        acc = buf(n, "acc")
        total = acc[y, z, x].astype(F32)
        for k, copy in enumerate(arrived[n]["z"]):
            copy.wait_recv()
            total = total + buf(n, "z")[k].astype(F32)
        results[n][...] = total

    small_at = [0]

    def small_stage(moves):
        copies = []
        for target in moves:
            slot = small_at[0]
            small_at[0] += 1
            copies.append((slot, wire.start(small_acc, small_recv.at[slot], target)))
        for slot, copy in copies:
            copy.wait_send()
            wire.sent = [other for other in wire.sent if other is not copy]
        for slot, copy in copies:
            copy.wait_recv()
            small_acc[...] += small_recv[slot]

    small_acc[...] = small[...]
    for n in range(count):
        stage_core(n)
    begin(0)
    small_stage([wire.to(y, 1 - c, z, x)])
    for turn in range(count + 3):
        if turn < count:
            stage_one(turn)
        if 0 <= turn - 1 < count:
            stage_two(turn - 1)
        if 0 <= turn - 2 < count:
            stage_three(turn - 2)
        if 0 <= turn - 3:
            stage_four(turn - 3)
        if turn == 0:
            small_stage([wire.to(y, c, z, (x + k) % X) for k in range(1, X)])
            small_stage([wire.to((y + k) % Y, c, z, x) for k in range(1, Y)])
            small_stage([wire.to(y, c, (z + k) % Z, x) for k in range(1, Z)])
            begin(1)
    small_out[...] = small_acc[...]
    wait(0)
    wait(1)
    wire.finish()


def scatter_all(lay, grads, small, blocks, rows, width):
    count = len(grads)
    X, Y, Z = lay.X, lay.Y, lay.Z
    out_count = len(blocks)
    micro = lay.MS // lay.items
    scratch = []
    outs = []
    for grad in grads:
        r, cols = grad.shape[-2:]
        left = half_columns(cols)
        right = cols - left if cols > left else LANES
        kind = grad.dtype
        scratch += [
            pltpu.VMEM((Y, Z, X, r, cols), kind),
            pltpu.VMEM((Y, Z, X, r, cols), kind),
            pltpu.VMEM((X - 1, Y, Z, r, left), kind),
            pltpu.VMEM((Y - 1, Z, X, r, right), kind),
            pltpu.VMEM((Y - 1, Z, r, left), kind),
            pltpu.VMEM((X - 1, Z, r, right), kind),
            pltpu.VMEM((Z - 1, r, cols), kind),
        ]
        outs.append(jax.ShapeDtypeStruct((r, cols), F32))
    hops = 1 + (X - 1) + (Y - 1) + (Z - 1)
    per = 1 + 2 * (X - 1 + Y - 1) + Z - 1
    outs.append(jax.ShapeDtypeStruct(small.shape, F32))
    outs += [jax.ShapeDtypeStruct((micro, lay.items, rows, width), b.dtype) for b in blocks]
    scratch += [pltpu.VMEM(small.shape, F32), pltpu.VMEM((hops,) + small.shape, F32)]
    scratch += [
        pltpu.SemaphoreType.DMA((count * per + hops,)),
        pltpu.SemaphoreType.DMA((count * per + hops,)),
        pltpu.SemaphoreType.DMA((count,)),
        pltpu.SemaphoreType.DMA((out_count, lay.BL)),
        pltpu.SemaphoreType.DMA((out_count, lay.MS)),
        pltpu.SemaphoreType.DMA((out_count,)),
    ]

    def body(*refs):
        scatter_kernel(lay, count, out_count, refs)

    result = pl.pallas_call(
        body,
        out_shape=outs,
        in_specs=[ANY] * count + [VM] + [ANY] * out_count,
        out_specs=[VM] * (count + 1) + [ANY] * out_count,
        scratch_shapes=scratch,
        compiler_params=pltpu.CompilerParams(
            collective_id=1, has_side_effects=True, vmem_limit_bytes=52 * 2**20
        ),
        name="scatter_all",
    )(*grads, small, *blocks)
    return result[:count], result[count], result[count + 1 :]


def row(ref, index, lanes):
    return jnp.broadcast_to(ref[pl.ds(index, 1), lanes], (SEG, LANES))


def lane_call(kernel, outs, args, name):
    def spec(a):
        lead = len(a.shape) - 1
        return pl.BlockSpec(a.shape[:-1] + (LANES,), lambda i: (0,) * lead + (i,))

    return pl.pallas_call(
        kernel,
        out_shape=outs,
        grid=(args[0].shape[-1] // LANES,),
        in_specs=[spec(a) for a in args],
        out_specs=jax.tree.map(spec, outs),
        compiler_params=pltpu.CompilerParams(vmem_limit_bytes=32 * 2**20),
        name=name,
    )(*args)


def shifted(value, by):
    where = lax.broadcasted_iota(jnp.int32, (SEG, LANES), 0)
    if by > 0:
        return jnp.where(where >= by, pltpu.roll(value, by, 0), 0.0)
    return jnp.where(where < SEG + by, pltpu.roll(value, SEG + by, 0), 0.0)


def ema_ends_kernel(H, x_ref, tab_ref, s_ref, r_ref):
    rows, width = x_ref.shape
    steps = rows // SEG

    def tile(lanes):
        decay = [row(tab_ref, h, lanes) for h in range(H)]

        def step(t, state):
            s, r = state
            xt = x_ref[pl.ds(t, SEG, stride=steps), lanes]
            r = tuple(decay[h] * r[h] + s[h] for h in range(H))
            s = tuple(decay[h] * s[h] + xt for h in range(H))
            return s, r

        zero = tuple(tab_ref[0:SEG, lanes] * 0.0 for h in range(H))
        s, r = lax.fori_loop(0, steps, step, (zero, zero))
        for h in range(H):
            log = row(tab_ref, H + h, lanes)
            sh, rh = s[h], r[h]
            for d in (1, 2, 4):
                span = d * steps
                sd, rd = shifted(sh, d), shifted(rh, d)
                power = jnp.exp(span * log)
                rh = rh + power * rd + (span * jnp.exp((span - 1) * log)) * sd
                sh = sh + power * sd
            s_ref[h, :, lanes] = sh
            r_ref[h, :, lanes] = rh

    tile(slice(None))


def ema_out_kernel(H, x_ref, tab_ref, omega_ref, s_ref, r_ref, inc_ref, ema_ref, mixed_ref, si_ref, ri_ref):
    rows, width = x_ref.shape
    steps = rows // SEG

    def tile(lanes):
        decay = [row(tab_ref, h, lanes) for h in range(H)]
        gain = [row(tab_ref, 2 * H + h, lanes) for h in range(H)]
        omega = row(omega_ref, 0, lanes)
        start = []
        span = (lax.broadcasted_iota(jnp.int32, (SEG, LANES), 0) * steps).astype(F32)
        for h in range(H):
            log = row(tab_ref, H + h, lanes)
            s_dev = jnp.broadcast_to(inc_ref[0, pl.ds(h, 1), lanes], (SEG, LANES))
            r_dev = jnp.broadcast_to(inc_ref[1, pl.ds(h, 1), lanes], (SEG, LANES))
            power = jnp.exp(span * log)
            s_in = shifted(s_ref[h, :, lanes], 1) + power * s_dev
            r_in = (
                shifted(r_ref[h, :, lanes], 1)
                + power * r_dev
                + (span * jnp.exp((span - 1.0) * log)) * s_dev
            )
            si_ref[h, :, lanes] = s_in
            ri_ref[h, :, lanes] = r_in
            start.append(s_in)

        def step(t, s):
            xt = x_ref[pl.ds(t, SEG, stride=steps), lanes]
            s = tuple(decay[h] * s[h] + xt for h in range(H))
            parts = [gain[h] * s[h] for h in range(H)]
            while len(parts) > 1:
                parts = [parts[i] + parts[i + 1] for i in range(0, len(parts), 2)]
            ema_ref[pl.ds(t, SEG, stride=steps), lanes] = parts[0] + omega * xt
            return s

        lax.fori_loop(0, steps, step, tuple(start))

    tile(slice(None))

    def finish(i, carry):
        at = pl.ds(pl.multiple_of(i * 64, 64), 64)
        value = ema_ref[at, :]
        mixed_ref[at, :] = (value * jax.nn.sigmoid(value)).astype(BF16)
        return carry

    lax.fori_loop(0, rows // 64, finish, 0)


def ema_back_ends_kernel(H, d_ref, tab_ref, l_ref):
    rows, width = d_ref.shape
    steps = rows // SEG

    def tile(lanes):
        decay = [row(tab_ref, h, lanes) for h in range(H)]

        def step(i, lam):
            dt = d_ref[pl.ds(steps - 1 - i, SEG, stride=steps), lanes]
            return tuple(decay[h] * lam[h] + dt for h in range(H))

        zero = tuple(tab_ref[0:SEG, lanes] * 0.0 for h in range(H))
        lam = lax.fori_loop(0, steps, step, zero)
        for h in range(H):
            log = row(tab_ref, H + h, lanes)
            lh = lam[h]
            for d in (1, 2, 4):
                lh = lh + jnp.exp(d * steps * log) * shifted(lh, -d)
            l_ref[h, :, lanes] = lh

    tile(slice(None))


def ema_sums_kernel(H, x_ref, d_ref, tab_ref, si_ref, ri_ref, out_ref):
    rows, width = x_ref.shape
    steps = rows // SEG
    group = H // 2

    def tile(lanes):
        for first in range(0, H, group):
            decay = [row(tab_ref, first + h, lanes) for h in range(group)]

            def step(t, state):
                s, r, c, q, o = state
                xt = x_ref[pl.ds(t, SEG, stride=steps), lanes]
                dt = d_ref[pl.ds(t, SEG, stride=steps), lanes]
                r = tuple(decay[h] * r[h] + s[h] for h in range(group))
                s = tuple(decay[h] * s[h] + xt for h in range(group))
                c = tuple(c[h] + dt * s[h] for h in range(group))
                q = tuple(q[h] + dt * r[h] for h in range(group))
                return s, r, c, q, o + dt * xt

            zero = tuple(tab_ref[0:SEG, lanes] * 0.0 for h in range(group))
            s = tuple(si_ref[first + h, :, lanes] for h in range(group))
            r = tuple(ri_ref[first + h, :, lanes] for h in range(group))
            s, r, c, q, o = lax.fori_loop(0, steps, step, (s, r, zero, zero, zero[0]))
            for h in range(group):
                out_ref[pl.ds(first + h, 1), lanes] = jnp.sum(c[h], axis=0, keepdims=True)
                out_ref[pl.ds(H + first + h, 1), lanes] = jnp.sum(q[h], axis=0, keepdims=True)
            out_ref[pl.ds(2 * H, 1), lanes] = jnp.sum(o, axis=0, keepdims=True)

    tile(slice(None))


def ema_back_kernel(H, d_ref, tab_ref, omega_ref, l_ref, inc_ref, dx_ref):
    rows, width = d_ref.shape
    steps = rows // SEG

    def tile(lanes):
        decay = [row(tab_ref, h, lanes) for h in range(H)]
        gain = [row(tab_ref, 2 * H + h, lanes) for h in range(H)]
        omega = row(omega_ref, 0, lanes)
        start = []
        span = ((SEG - 1 - lax.broadcasted_iota(jnp.int32, (SEG, LANES), 0)) * steps).astype(F32)
        for h in range(H):
            log = row(tab_ref, H + h, lanes)
            l_dev = jnp.broadcast_to(inc_ref[pl.ds(h, 1), lanes], (SEG, LANES))
            start.append(shifted(l_ref[h, :, lanes], -1) + jnp.exp(span * log) * l_dev)

        def step(i, lam):
            at = pl.ds(steps - 1 - i, SEG, stride=steps)
            dt = d_ref[at, lanes]
            lam = tuple(decay[h] * lam[h] + dt for h in range(H))
            parts = [gain[h] * lam[h] for h in range(H)]
            while len(parts) > 1:
                parts = [parts[i] + parts[i + 1] for i in range(0, len(parts), 2)]
            dx_ref[at, lanes] = parts[0] + omega * dt
            return lam

        lax.fori_loop(0, steps, step, tuple(start))

    tile(slice(None))


def call(kernel, outs, args, specs=None, scratch=(), vmem=58, name=None):
    return pl.pallas_call(
        kernel,
        out_shape=outs,
        in_specs=specs or [VM] * len(args),
        out_specs=jax.tree.map(lambda o: VM, outs),
        scratch_shapes=list(scratch),
        compiler_params=pltpu.CompilerParams(vmem_limit_bytes=vmem * 2**20),
        name=name,
    )(*args)


QB = 256


def bias_kernel(length, bucket_count, bias_ref, strip_ref):
    edges = bucket_edges(bucket_count)
    tiles = length // LANES + QB // LANES
    lag0 = lax.broadcasted_iota(jnp.int32, (QB, LANES), 0) - lax.broadcasted_iota(
        jnp.int32, (QB, LANES), 1
    )
    for t in range(strip_ref.shape[1] // LANES):
        base = length - t * LANES
        low, high = base - LANES + 1, base + QB - 1
        start = max([k for k in range(bucket_count) if edges[k] <= low], default=0)
        value = jnp.full((QB, LANES), bias_ref[start], F32)
        for k in range(start + 1, bucket_count):
            if edges[k] <= high:
                value = jnp.where(lag0 + base >= edges[k], bias_ref[k], value)
        strip_ref[:, t * LANES : (t + 1) * LANES] = value


def attend_kernel(lay, flag_ref, q_ref, strip_ref, *refs):
    G = lay.G
    keys, vals = refs[:G], refs[G : 2 * G]
    att_ref, probs_ref, scores = refs[2 * G :]
    rows, zw = q_ref.shape
    length = G * rows
    full = flag_ref[0] > 0
    g = flag_ref[1]
    r0 = lax.broadcasted_iota(jnp.int32, (QB, rows), 0)
    c0 = lax.broadcasted_iota(jnp.int32, (QB, rows), 1)

    def one(i, carry):
        at = pl.multiple_of(i * QB, QB)
        q = q_ref[pl.ds(at, QB), :]
        for k in range(G):
            owner = lax.rem(g - k + G, G)
            s = lax.dot_general(q, keys[k][...], (((1,), (1,)), ((), ())), preferred_element_type=F32)
            off = jnp.clip(length - rows * (g - owner) - at, 0, length)
            s = s * (zw ** (-0.5)) + strip_ref[:, pl.ds(pl.multiple_of(off, LANES), rows)]
            if k == 0:
                pos = r0 + at
                ok = (c0 <= pos) & (full | (pos // 128 == c0 // 128))
            else:
                ok = jnp.logical_and(full, k <= g)
            scores[:, k * rows : (k + 1) * rows] = jnp.where(ok, s, masked_fill)
        s = scores[...]
        p = jnp.exp(s - jnp.max(s, axis=1, keepdims=True))
        p = p * (1.0 / jnp.sum(p, axis=1, keepdims=True))
        total = jnp.zeros((QB, att_ref.shape[1]), F32)
        for k in range(G):
            part = p[:, k * rows : (k + 1) * rows]
            probs_ref[k, pl.ds(at, QB), :] = part
            total += jnp.dot(part.astype(BF16), vals[k][...], preferred_element_type=F32)
        att_ref[pl.ds(at, QB), :] = total
        return carry

    lax.fori_loop(0, rows // QB, one, 0)


def attend_back_kernel(lay, bucket_count, flag_ref, q_ref, da_ref, delta_ref, probs_ref, *refs):
    G = lay.G
    keys, vals = refs[:G], refs[G : 2 * G]
    dq_ref, dk_ref, dv_ref, dko_ref, dvo_ref, bucket_ref, strip, ds_ref, pb_ref = refs[2 * G :]
    rows, zw = q_ref.shape
    length = G * rows
    g = flag_ref[1]
    scale = zw ** (-0.5)
    edges = bucket_edges(bucket_count)
    strip[...] = jnp.zeros(strip.shape, F32)

    def one(i, carry):
        at = pl.multiple_of(i * QB, QB)
        da = da_ref[pl.ds(at, QB), :]
        dq = jnp.zeros((QB, zw), F32)
        for k in range(G):
            owner = lax.rem(g - k + G, G)
            dw = lax.dot_general(da, vals[k][...], (((1,), (1,)), ((), ())), preferred_element_type=F32)
            p = probs_ref[k, pl.ds(at, QB), :]
            ds = p * (dw - delta_ref[pl.ds(at, QB), :])
            off = jnp.clip(length - rows * (g - owner) - at, 0, length)
            strip[:, pl.ds(pl.multiple_of(off, LANES), rows)] += ds
            low = ds.astype(BF16)
            dq += jnp.dot(low, keys[k][...], preferred_element_type=F32)
            ds_ref[k, pl.ds(at, QB), :] = low
            pb_ref[k, pl.ds(at, QB), :] = p.astype(BF16)
        dq_ref[pl.ds(at, QB), :] = dq * scale
        return carry

    lax.fori_loop(0, rows // QB, one, 0)
    for k in range(G):
        dk = lax.dot_general(
            ds_ref[k], q_ref[...], (((0,), (0,)), ((), ())), preferred_element_type=F32
        )
        dv = lax.dot_general(
            pb_ref[k], da_ref[...], (((0,), (0,)), ((), ())), preferred_element_type=F32
        )
        if k == 0:
            dk_ref[...] = dk * scale
            dv_ref[...] = dv
        else:
            dko_ref[k - 1] = (dk * scale).astype(BF16)
            dvo_ref[k - 1] = dv.astype(BF16)
    lag0 = lax.broadcasted_iota(jnp.int32, (QB, LANES), 0) - lax.broadcasted_iota(
        jnp.int32, (QB, LANES), 1
    )
    sums = [jnp.zeros((1, LANES), F32) for k in range(bucket_count)]
    for t in range((length + QB) // LANES):
        base = length - t * LANES
        low, high = base - LANES + 1, base + QB - 1
        if high < 0:
            continue
        value = strip[:, t * LANES : (t + 1) * LANES]
        for k in range(bucket_count):
            top = edges[k + 1] if k + 1 < bucket_count else length
            if edges[k] <= high and top > low:
                lag = lag0 + base
                inside = (lag >= edges[k]) & (lag < top)
                sums[k] = sums[k] + jnp.sum(jnp.where(inside, value, 0.0), axis=0, keepdims=True)
    for k in range(bucket_count):
        bucket_ref[pl.ds(k, 1), :] = sums[k]


def silu_slope(values):
    gate_value = jax.nn.sigmoid(values)
    return gate_value * (1.0 + values * (1.0 - gate_value))


def normalize(seq_rows):
    centered = seq_rows - jnp.mean(seq_rows, axis=-1, keepdims=True)
    inverse = lax.rsqrt(jnp.mean(centered * centered, axis=-1, keepdims=True) + epsilon)
    return (centered * inverse, inverse)


def normalize_back(grad_scaled, unit_rows, inverse):
    return inverse * (
        grad_scaled
        - jnp.mean(grad_scaled, axis=-1, keepdims=True)
        - unit_rows * jnp.mean(grad_scaled * unit_rows, axis=-1, keepdims=True)
    )


def mm(a, b):
    return jnp.dot(a, b, preferred_element_type=F32)


def mm_t(a, b):
    return lax.dot_general(a, b, (((1,), (1,)), ((), ())), preferred_element_type=F32)


def wgrad(a, b):
    return lax.dot_general(a, b, (((0,), (0,)), ((), ())), preferred_element_type=F32).astype(BF16)


def shards(
    lay,
    tokens,
    cotangent,
    stretch_size,
    w_value,
    w_base,
    w_out,
    w_up,
    w_down,
    ema_delta,
    ema_alpha,
    ema_beta,
    ema_gamma,
    ema_omega,
    first_gain,
    second_gain,
    query_gain,
    query_bias,
    key_gain,
    relative_bias,
):
    micro, items, seq_len, D = tokens.shape
    H = ema_delta.shape[1]
    zw = query_gain.shape[0]
    V = w_value.shape[1]
    NB = relative_bias.shape[0]
    length = seq_len * lay.S
    G = lay.G
    R = lay.BL * seq_len
    d_at, b_at = lax.axis_index("dp"), lax.axis_index("seq")
    c_at, y_at = d_at % 2, d_at // 2
    q_at = b_at // lay.Cq
    g_at = (b_at % lay.Cq) * 2 + c_at
    share = ema_delta.shape[0]

    def group_perm(k):
        pairs = []
        for y in range(lay.Y):
            for q in range(lay.Q):
                for g in range(G):
                    t = (g + k) % G
                    src = (y * 2 + g % 2) * lay.S + q * lay.Cq + g // 2
                    dst = (y * 2 + t % 2) * lay.S + q * lay.Cq + t // 2
                    pairs.append((src, dst))
        return pairs

    def shift(value, k):
        return lax.ppermute(value, ("dp", "seq"), group_perm(k % G))

    marks = jnp.broadcast_to(
        stretch_size.reshape(1, -1).astype(BF16), (share, lay.MS)
    )
    used = 4 * H + 3 + lay.MS
    pack = jnp.concatenate(
        [
            ema_delta,
            ema_alpha,
            ema_beta,
            ema_gamma,
            ema_omega[:, None],
            first_gain[:, None],
            second_gain[:, None],
            marks,
            jnp.zeros((share, LANES - used), BF16),
        ],
        1,
    )
    x_blocks, cot_blocks, fulls = gather_all(
        lay, tokens, cotangent, (pack, w_value, w_base, w_out, w_up, w_down)
    )
    pack_full = fulls[0]
    mark = pack_full[y_at, q_at % 2, 0, 0, 0, 4 * H + 3 + q_at // 2]
    flags = jnp.stack([(mark.astype(jnp.int32) == length).astype(jnp.int32), g_at])
    mats = [full.reshape(D if full.shape[-2] == share else -1, full.shape[-1]) for full in fulls[1:]]
    mat_value, mat_base, mat_out, mat_up, mat_down = mats
    raw = pack_full.reshape(D, LANES).astype(F32).T
    leak = jax.nn.sigmoid(raw[:H])
    decay = 1.0 - leak * jax.nn.sigmoid(raw[H : 2 * H])
    log_decay = jnp.log(decay)
    gain = leak * raw[2 * H : 3 * H] * raw[3 * H : 4 * H] * (H ** (-0.5))
    table = jnp.concatenate([decay, log_decay, gain])
    omega = raw[4 * H : 4 * H + 1]
    gain_first = raw[4 * H + 1]
    gain_second = raw[4 * H + 2]

    x_low = x_blocks.reshape(R, D)
    x = x_low.astype(F32)
    grad_out = cot_blocks.reshape(R, D).astype(F32)

    state = jax.ShapeDtypeStruct((H, SEG, D), F32)
    ends_s, ends_r = lane_call(
        functools.partial(ema_ends_kernel, H), [state, state], (x, table), name="ema_ends"
    )
    mine = jnp.stack([ends_s[:, SEG - 1], ends_r[:, SEG - 1]])
    inc = jnp.zeros_like(mine)
    for k in range(1, G):
        other = shift(mine, k)
        span = (k - 1) * R
        s_part, r_part = other[0], other[1]
        if span:
            power = jnp.exp(span * log_decay)
            r_part = power * r_part + span * jnp.exp((span - 1) * log_decay) * s_part
            s_part = power * s_part
        inc = inc + jnp.where(k <= g_at, jnp.stack([s_part, r_part]), 0.0)
    value_pre = mm(x_low, mat_value)
    values = jax.nn.silu(value_pre).astype(BF16)
    ema, mixed, s_in, r_in = lane_call(
        functools.partial(ema_out_kernel, H),
        [jax.ShapeDtypeStruct((R, D), F32), jax.ShapeDtypeStruct((R, D), BF16), state, state],
        (x, table, omega, ends_s, ends_r, inc),
        name="ema_out",
    )
    base = mm(mixed, mat_base)
    z_pre = base[:, :zw]
    reset_pre = base[:, zw : zw + V]
    cand_pre = base[:, zw + V : zw + V + D]
    update_pre = base[:, zw + V + D :]
    shared = jax.nn.silu(z_pre)
    queries = (shared * query_gain + query_bias).astype(BF16)
    keys = (shared * key_gain).astype(BF16)
    keys_all = [keys] + [shift(keys, k) for k in range(1, G)]
    vals_all = [values] + [shift(values, k) for k in range(1, G)]
    strip = call(
        functools.partial(bias_kernel, length, NB),
        jax.ShapeDtypeStruct((QB, length + R), F32),
        (relative_bias,),
        specs=[SM],
        name="bias_strip",
    )
    attended, probs = call(
        functools.partial(attend_kernel, lay),
        [jax.ShapeDtypeStruct((R, V), F32), jax.ShapeDtypeStruct((G, R, R), F32)],
        (flags, queries, strip, *keys_all, *vals_all),
        specs=[SM] + [VM] * (2 + 2 * G),
        scratch=[pltpu.VMEM((QB, length), F32)],
        name="attend",
    )
    reset_gate = jax.nn.silu(reset_pre)
    update = jax.nn.sigmoid(update_pre)
    gated = (attended * reset_gate).astype(BF16)
    cand_in = cand_pre + mm(gated, mat_out)
    candidate = jax.nn.silu(cand_in)
    first_sum = x + update * (candidate - x)
    unit_first, inverse_first = normalize(first_sum)
    normed = unit_first * gain_first
    normed_low = normed.astype(BF16)
    hidden_pre = mm(normed_low, mat_up)
    hidden = jax.nn.silu(hidden_pre).astype(BF16)
    second_sum = normed + mm(hidden, mat_down)
    unit_second, inverse_second = normalize(second_sum)
    block_out = (unit_second * gain_second).astype(BF16)

    grad_gain_second = jnp.sum(grad_out * unit_second, axis=0)
    grad_second = normalize_back(grad_out * gain_second, unit_second, inverse_second)
    branch = grad_second.astype(BF16)
    grad_mat_down = wgrad(hidden, branch)
    hidden_grad = (mm_t(branch, mat_down) * silu_slope(hidden_pre)).astype(BF16)
    grad_mat_up = wgrad(normed_low, hidden_grad)
    grad_normed = grad_second + mm_t(hidden_grad, mat_up)
    grad_gain_first = jnp.sum(grad_normed * unit_first, axis=0)
    grad_first = normalize_back(grad_normed * gain_first, unit_first, inverse_first)
    cand_low = (grad_first * update * silu_slope(cand_in)).astype(BF16)
    grad_mat_out = wgrad(gated, cand_low)
    grad_gated = mm_t(cand_low, mat_out)
    att_low = (grad_gated * reset_gate).astype(BF16)
    grad_reset = grad_gated * attended * silu_slope(reset_pre)
    grad_update = grad_first * (candidate - x) * update * (1.0 - update)
    delta = jnp.sum(att_low.astype(F32) * attended, axis=1, keepdims=True)
    dq, grad_keys, grad_values, dk_out, dv_out, buckets = call(
        functools.partial(attend_back_kernel, lay, NB),
        [
            jax.ShapeDtypeStruct((R, zw), F32),
            jax.ShapeDtypeStruct((R, zw), F32),
            jax.ShapeDtypeStruct((R, V), F32),
            jax.ShapeDtypeStruct((G - 1, R, zw), BF16),
            jax.ShapeDtypeStruct((G - 1, R, V), BF16),
            jax.ShapeDtypeStruct((NB, LANES), F32),
        ],
        (flags, queries, att_low, delta, probs, *keys_all, *vals_all),
        specs=[SM] + [VM] * (4 + 2 * G),
        scratch=[
            pltpu.VMEM((QB, length + R), F32),
            pltpu.VMEM((G, R, R), BF16),
            pltpu.VMEM((G, R, R), BF16),
        ],
        name="attend_back",
    )
    for k in range(1, G):
        grad_keys = grad_keys + shift(dk_out[k - 1], -k).astype(F32)
        grad_values = grad_values + shift(dv_out[k - 1], -k).astype(F32)
    grad_query_gain = jnp.sum(dq * shared, axis=0)
    grad_query_bias = jnp.sum(dq, axis=0)
    grad_key_gain = jnp.sum(grad_keys * shared, axis=0)
    grad_relative = jnp.sum(buckets, axis=1)
    grad_z = (dq * query_gain + grad_keys * key_gain) * silu_slope(z_pre)
    base_low = jnp.concatenate(
        [grad_z.astype(BF16), grad_reset.astype(BF16), cand_low, grad_update.astype(BF16)], 1
    )
    grad_mat_base = wgrad(mixed, base_low)
    grad_ema = mm_t(base_low, mat_base) * silu_slope(ema)
    lam_ends = lane_call(
        functools.partial(ema_back_ends_kernel, H), state, (grad_ema, table), name="ema_back_ends"
    )
    lam_mine = lam_ends[:, 0]
    lam_inc = jnp.zeros_like(lam_mine)
    for k in range(1, G):
        part = shift(lam_mine, -k)
        span = (k - 1) * R
        if span:
            part = jnp.exp(span * log_decay) * part
        lam_inc = lam_inc + jnp.where(g_at + k < G, part, 0.0)
    ema_sums = lane_call(
        functools.partial(ema_sums_kernel, H),
        jax.ShapeDtypeStruct((2 * H + 8, D), F32),
        (x, grad_ema, table, s_in, r_in),
        name="ema_sums",
    )
    value_low = (grad_values * silu_slope(value_pre)).astype(BF16)
    grad_mat_value = wgrad(x_low, value_low)
    grad_x_value = mm_t(value_low, mat_value)
    grad_x_ema = lane_call(
        functools.partial(ema_back_kernel, H),
        jax.ShapeDtypeStruct((R, D), F32),
        (grad_ema, table, omega, lam_ends, lam_inc),
        name="ema_back",
    )
    grad_x = (grad_first * (1.0 - update) + grad_x_ema + grad_x_value).astype(BF16)

    sums = jnp.concatenate(
        [
            ema_sums[: 2 * H + 1],
            grad_gain_first[None],
            grad_gain_second[None],
            jnp.zeros((LANES - 2 * H - 3, D), F32),
        ]
    ).T
    small = jnp.zeros((8, LANES), F32)
    small = small.at[0, :zw].set(grad_query_gain)
    small = small.at[1, :zw].set(grad_query_bias)
    small = small.at[2, :zw].set(grad_key_gain)
    small = small.at[3, :NB].set(grad_relative)
    shape = (lay.Y, 2, lay.Z, lay.X)

    def split(grad):
        return grad.reshape(shape + (-1, grad.shape[-1]))

    reduced, small_total, moved = scatter_all(
        lay,
        [
            split(grad_mat_down),
            split(grad_mat_up),
            split(grad_mat_out),
            split(grad_mat_base),
            split(grad_mat_value),
            split(sums),
        ],
        small,
        [block_out.reshape(lay.BL, seq_len, D), grad_x.reshape(lay.BL, seq_len, D)],
        seq_len,
        D,
    )
    own = reduced[5]
    corr, lagged = own[:, :H], own[:, H : 2 * H]
    p = jax.nn.sigmoid(ema_delta.astype(F32))
    a = jax.nn.sigmoid(ema_alpha.astype(F32))
    beta = ema_beta.astype(F32)
    read = ema_gamma.astype(F32) * (H ** (-0.5))
    q_grad = read * p * beta * lagged
    return (
        moved[0],
        moved[1].astype(F32),
        reduced[4],
        reduced[3],
        reduced[2],
        reduced[1],
        reduced[0],
        (read * beta * corr - a * q_grad) * p * (1.0 - p),
        -p * q_grad * a * (1.0 - a),
        p * read * corr,
        p * beta * corr * (H ** (-0.5)),
        own[:, 2 * H],
        own[:, 2 * H + 1],
        own[:, 2 * H + 2],
        small_total[0, :zw],
        small_total[1, :zw],
        small_total[2, :zw],
        small_total[3, :NB],
    )


def solution(mesh):
    rows = P(None, "dp", "seq", None)
    part2, part1 = P(("dp", "seq"), None), P(("dp", "seq"))
    in_specs = (rows, rows, P(None, "dp")) + (part2,) * 9 + (part1,) * 3 + (P(),) * 4
    out_specs = (rows, rows) + (part2,) * 9 + (part1,) * 3 + (P(),) * 4

    def whole(tokens, *rest):
        micro, seqs = tokens.shape[:2]
        lay = Layout(mesh.shape["dp"], mesh.shape["seq"], micro, seqs // mesh.shape["dp"])
        return jax.shard_map(
            functools.partial(shards, lay),
            mesh=mesh,
            in_specs=in_specs,
            out_specs=out_specs,
            check_vma=False,
        )(tokens, *rest)

    return whole
```

time: 2960 us -> 442 us (0.15)
  matrix products: 1150 us -> 55.5 us
  waiting for transfers between devices: 723 us -> 0.02 us
  blocking collectives: 657 us -> 0 us
  Pallas kernels: 0 us -> 308 us
  local copies, waits for them, and re-layouts: 205 us -> 43.2 us
  other arithmetic: 150 us -> 23 us
  loops' own time: 33.1 us -> 0 us
    dot_general x129 -> x15, matrix products: 1150 us -> 55.5 us  [the longest x5 19.2 us: wgrad(): lax.dot_general(a, b, (((0,), (0,)), ((), ())), preferred_element_type=F32)]
    all_gather x15 -> x0, blocking collectives: 620 us -> none  [the longest x5 164 us: carried_in(): pieces = jax.tree.map(lambda part: lax.all_gather(part, axis), value)]
    unnamed x18 -> x0, waiting for transfers between devices: 335 us -> none
    reduce_scatter x3 -> x0, waiting for transfers between devices: 331 us -> none  [the longest x1 113 us: shards(): lax.psum_scatter(full_grads[2], ('dp', 'seq'), scatter_dimension=0, tiled...]
    pallas_call x0 -> x10, Pallas kernels: none -> 308 us  [the longest x1 129 us: gather_all(): pl.pallas_call(body, out_shape=outs, in_specs=[ANY] * (2 + count), out_sp...]
    all_gather x9 -> x0, waiting for transfers between devices: 57.4 us -> none  [the longest x1 55.6 us: shards(): lax.all_gather(w_down, ('dp', 'seq'), axis=0, tiled=True)]
    unnamed x584 -> x171, local copies, waits for them, and re-layouts: 79.2 us -> 32.5 us
    reduce_sum x15 -> x3, other arithmetic: 48.4 us -> 3.93 us  [the longest x1 1.68 us: shards(): grad_key_gain = jnp.sum(grad_keys * shared, axis=0)]
  transfers between devices with their start and end apart: 15 -> 6, of which waited for: 8 -> 0; matrix products, arithmetic and copies ran while one was open for 25% -> 9% of each run, Pallas kernels for 0% -> 10%
where the time goes in v1:
time: 442 us; the launch traced here: 435 us
  Pallas kernels  308 us (70%)
  matrix products  55.5 us (13%)
  local copies, waits for them, and re-layouts  43.2 us (10%)
  other arithmetic  23 us (5%)
    pallas_call x1, Pallas kernels, gather_all(): pl.pallas_call(body, out_shape=outs, in_specs=[ANY] * (2 + count), out_sp...  129 us
    pallas_call x1, Pallas kernels, scatter_all(): pl.pallas_call(body, out_shape=outs, in_specs=[ANY] * count + [VM] + [ANY...  107 us
    pallas_call x5, Pallas kernels, lane_call(): pl.pallas_call(kernel, out_shape=outs, grid=(args[0].shape[-1] // LANES,)...  52.5 us
    unnamed x171, local copies, waits for them, and re-layouts  32.5 us
    pallas_call x3, Pallas kernels, call(): pl.pallas_call(kernel, out_shape=outs, in_specs=specs or [VM] * len(args)...  19.3 us
    dot_general x5, matrix products, wgrad(): lax.dot_general(a, b, (((0,), (0,)), ((), ())), preferred_element_type=F32)  19.2 us
    dot_general x5, matrix products, mm(): return jnp.dot(a, b, preferred_element_type=F32)  18.2 us
    dot_general x5, matrix products, mm_t(): lax.dot_general(a, b, (((1,), (1,)), ((), ())), preferred_element_type=F32)  18 us
  transfers between devices with their start and end apart: 6, of which 0 were waited for; matrix products, arithmetic and copies ran while one was open for 9% of the time, Pallas kernels for 10%

profile of v1, /device:TPU:0, one launch (start us, length us, event | category | flops | bytes accessed | tf_op | source)
XLA Modules:
  0.0 434.6 jit_solution(17449865750085147007)
XLA Ops:
  13.6 128.5 %gather_all.1 = (bf16[4,128,768]{2,1,0:T(8,128)(2,1)S(1)}, bf16[4,128,768]{2,1,0:T(8,128)(2,1)S(1)}, bf16[2,2,4,2,24,128]{5,4,3,2,1,0:T(8,128)(2,1)S(1)}, bf16[2...) custom-call(bf16[2,2,128,768]{3,2,1,0:T(8,128)(2,1)S(1)} %copy-done., ...), custom_call_target="tpu_custom_call" | custom-call | tf_op jit(solution)/shard_map/gather_all/pallas_call | solution.py:344
  142.2 2.2 copy-done
  151.3 9.4 %ema_ends.1 = (f32[16,8,768]{2,1,0:T(8,128)S(1)}, f32[16,8,768]{2,1,0:T(8,128)S(1)}) custom-call(f32[512,768]{1,0:T(8,128)S(1)} %bitcast_convert_fusion.1.x_ref, f32[48,768]{1,0:T(8,128)S(1)} %pad_maximum_fusion.3.tab_ref), custom_call_target="tpu_custom_call" | custom-call | tf_op jit(solution)/shard_map/ema_ends/pallas_call | solution.py:622
  162.1 4.0 multiply_convert_fusion.5
  169.3 10.3 %ema_out.1 = (f32[512,768]{1,0:T(8,128)S(1)}, bf16[512,768]{1,0:T(8,128)(2,1)S(1)}, f32[16,8,768]{2,1,0:T(8,128)S(1)}, f32[16,8,768]{2,1,0:T(8,128)S(1)}) custom-call(f32[512,768]{1,0:T(8,128)S(1)} %bitcast_convert_fusion.1.x_ref, f32[48,768]{1,0:T(8,128)S(1)} %pad_maximum_fusion.3.tab_ref, f32[1,768]{1,0:T(1,128)S(1)} %get-tuple-element.208.omega_ref, ...), custom_call_target="tpu_custom_call" | custom-call | tf_op jit(solution)/shard_map/ema_out/pallas_call | solution.py:622
  179.7 6.4 %fusion.39 = f32[512,3200]{1,0:T(8,128)S(1)} fusion(bf16[512,768]{1,0:T(8,128)(2,1)S(1)} %get-tuple-element.101, bf16[768,3200]{1,0:T(8,128)(2,1)} %bitcast.95), kind=kOutput, calls=%fused_computation.127 | convolution fusion | flops 2516582400 | bytes 12255232 | tf_op jit(solution)/shard_map/dot_general | solution.py:956
  187.1 1.9 copy-done.31
  192.3 2.2 bias_strip.1.strip_ref
  195.7 7.4 %attend.1 = (f32[512,1536]{1,0:T(8,128)}, f32[2,512,512]{2,1,0:T(8,128)}) custom-call(s32[2]{0:T(128)} %pad_add_fusion.flag_ref, bf16[512,128]{1,0:T(8,128)(2,1)} %get-tuple-element.206.q_ref, f32[256,1536]{1,0:T(8,128)} %bias_strip.1.strip_ref, bf16[512,128]{1,0:T(8,128)(2,1)} %get-tuple-element.205.refs_0_, ...), custom_call_target="tpu_custom_call" | custom-call | tf_op jit(solution)/shard_map/attend/pallas_call | solution.py:803
  203.1 3.9 multiply_convert_fusion.4
  207.0 4.5 %fusion.34 = (f32[512]{0:T(512)S(1)}, f32[512,768]{1,0:T(8,128)S(1)}, f32[512,768]{1,0:T(8,128)S(1)}) fusion(f32[512,3200]{1,0:T(8,128)} %copy-done.31, bf16[4,128,768]{2,1,0:T(8,128)(2,1)S(1)} %get-tuple-element.97, bf16[512,1536]{1,0:T(8,128)(2,1)S(1)} %multiply_convert_fusion.4, bf16[1536,768]{1,0:T(8,128)(2,1)S(1)} %bitcast.103), kind=kOutput, calls=%fused_computation.123 | convolution fusion | flops 1213070848 | bytes 11012096 | tf_op jit(solution)/shard_map/dot_general | solution.py:956
  213.7 1.9 fusion.38
  216.0 1.6 fusion.11
  218.1 1.9 fusion.1
  220.0 1.8 multiply_reduce_fusion.1
  221.8 3.0 convolution_convert_fusion.3
  224.7 3.1 convolution_convert_fusion.4
  227.9 2.7 multiply_convert_fusion.7
  230.7 3.8 multiply_reduce_fusion
  235.3 9.7 %attend_back.1 = (f32[512,128]{1,0:T(8,128)}, f32[512,128]{1,0:T(8,128)}, f32[512,1536]{1,0:T(8,128)}, bf16[1,512,128]{2,1,0:T(8,128)(2,1)}, bf16[1,512,1536]{2,1,0:T(8,128)(2,1)}, /*index=5*/f32[32,128]{1,0:T(8,128)}) custom-call(s32[2]{0:T(128)} %pad_add_fusion.flag_ref, bf16[512,128]{1,0:T(8,128)(2,1)} %get-tuple-element.206.q_ref, ...), custom_call_target="tpu_custom_call" | custom-call | tf_op jit(solution)/shard_map/attend_back/pallas_call | solution.py:803
  245.2 2.9 convolution_convert_fusion.2
  251.1 1.7 multiply_reduce_fusion.6
  252.8 6.6 %multiply_multiply_fusion.d_ref = f32[512,768]{1,0:T(8,128)S(1)} fusion(f32[512,768]{1,0:T(8,128)} %copy-done.30, bf16[768,3200]{1,0:T(8,128)(2,1)} %bitcast.96, bf16[512,768]{1,0:T(8,128)(2,1)} %get-tuple-element.202, bf16[512,768]{1,0:T(8,128)(2,1)S(1)} %copy-done.46, bf16[512,1536]{1,0:T(8,128)(2,1)} %get-tuple-element.201, ...), kind=kOutput, calls=%fused_computation.37 | convolution fusion | flops 2532835328 | bytes 11337728 | tf_op jit(solution)/shard_map/dot_general | solution.py:960
  259.3 6.7 %ema_back_ends.1.l_ref = f32[16,8,768]{2,1,0:T(8,128)S(1)} custom-call(f32[512,768]{1,0:T(8,128)S(1)} %multiply_multiply_fusion.d_ref, f32[48,768]{1,0:T(8,128)S(1)} %pad_maximum_fusion.3.tab_ref), custom_call_target="tpu_custom_call" | custom-call | tf_op jit(solution)/shard_map/ema_back_ends/pallas_call | solution.py:622
  267.5 16.5 %ema_sums.1 = f32[40,768]{1,0:T(8,128)S(1)} custom-call(f32[512,768]{1,0:T(8,128)S(1)} %bitcast_convert_fusion.1.x_ref, f32[512,768]{1,0:T(8,128)S(1)} %multiply_multiply_fusion.d_ref, f32[48,768]{1,0:T(8,128)S(1)} %pad_maximum_fusion.3.tab_ref, f32[16,8,768]{2,1,0:T(8,128)S(1)} %copy-done.13, f32[16,8,768]{2,1,0:T(8,128)S(1)} %copy-done.15), custom_call_target="tpu_custom_call" | custom-call | tf_op jit(solution)/shard_map/ema_sums/pallas_call | solution.py:622
  285.0 7.3 %convolution_convert_fusion = bf16[768,3200]{1,0:T(8,128)(2,1)} fusion(bf16[512,768]{1,0:T(8,128)(2,1)} %copy-done.9, bf16[512,768]{1,0:T(8,128)(2,1)} %get-tuple-element.202, bf16[512,768]{1,0:T(8,128)(2,1)} %copy-done.45, bf16[512,1536]{1,0:T(8,128)(2,1)} %get-tuple-element.201, bf16[512,128]{1,0:T(8,128)(2,1)S(1)} %get-tuple-element.204), kind=kOutput, calls=%fused_computation | convolution fusion | flops 2532147200 | bytes 8978432 | tf_op jit(solution)/shard_map/dot_general | solution.py:964
  295.0 9.6 %ema_back.1 = f32[512,768]{1,0:T(8,128)S(1)} custom-call(f32[512,768]{1,0:T(8,128)S(1)} %multiply_multiply_fusion.d_ref, f32[48,768]{1,0:T(8,128)S(1)} %pad_maximum_fusion.3.tab_ref, f32[1,768]{1,0:T(1,128)S(1)} %get-tuple-element.208.omega_ref, f32[16,8,768]{2,1,0:T(8,128)S(1)} %copy-done.4, f32[16,768]{1,0:T(8,128)S(1)} %broadcast_select_fusion.1.inc_ref), custom_call_target="tpu_custom_call" | custom-call | tf_op jit(solution)/shard_map/ema_back/pallas_call | solution.py:622
  304.7 3.8 multiply_convert_fusion
  308.6 2.8 convolution_convert_fusion.1
  311.5 4.0 add_convert_fusion
  315.5 107.4 %scatter_all.1 = (f32[48,768]{1,0:T(8,128)S(1)}, f32[24,1536]{1,0:T(8,128)S(1)}, f32[48,768]{1,0:T(8,128)S(1)}, f32[24,3200]{1,0:T(8,128)S(1)}, f32[24,1536]{1,0...) custom-call(bf16[2,2,4,2,48,768]{5,4,3,2,1,0:T(8,128)(2,1)} %bitcast, ...), custom_call_target="tpu_custom_call" | custom-call | tf_op jit(solution)/shard_map/scatter_all/pallas_call | solution.py:599
  424.0 2.4 convert_element_type.152
  (236 shorter events, 50.1 us)
Async XLA Ops:
  150.1 77.8 %copy-start.1 = (bf16[4,128,768]{2,1,0:T(8,128)(2,1)}, bf16[4,128,768]{2,1,0:T(8,128)(2,1)S(1)}, u32[]{:S(2)}) copy-start(bf16[4,128,768]{2,1,0:T(8,128)(2,1)S(1)} %get-tuple-element.97) | copy-start | bytes 2359300
  151.3 10.9 %copy-start.22 = (bf16[2,2,4,2,24,1536]{5,4,3,2,1,0:T(8,128)(2,1)S(1)}, bf16[2,2,4,2,24,1536]{5,4,3,2,1,0:T(8,128)(2,1)}, u32[]{:S(2)}) copy-start(bf16[2,2,4,2,24,1536]{5,4,3,2,1,0:T(8,128)(2,1)} %copy-done.21) | copy-start | bytes 7077892
  161.6 5.6 %collective-permute-start = (f32[2,16,768]{2,1,0:T(8,128)}, f32[2,16,768]{2,1,0:T(8,128)}, u32[]{:S(2)}, u32[]{:S(2)}) collective-permute-start(f32[2,16,768]{2,1,0:T(8,128)} %pad_maximum_fusion.4), channel_id=1, source_target_pairs={{0,8},{8,0},{1,9},{9,1},{2,10},{10,2},{3,11},{11,3},{4,12},{12,4},... | collective-permute-start | bytes 294920 | tf_op jit(solution)/shard_map/ppermute | solution.py:1015
  166.1 29.5 %collective-permute-start.2 = (bf16[512,1536]{1,0:T(8,128)(2,1)}, bf16[512,1536]{1,0:T(8,128)(2,1)}, u32[]{:S(2)}, u32[]{:S(2)}) collective-permute-start(bf16[512,1536]{1,0:T(8,128)(2,1)} %get-tuple-element.217.refs_2_), channel_id=1, source_target_pairs={{0,8},{8,0},{1,9},{9,1},{2,10},{10,2},{3,11},{11,3},{4,12},{12,4},... | collective-permute-start | bytes 4718600 | tf_op jit(solution)/shard_map/ppermute | solution.py:1015
  167.0 60.9 %copy-start.56 = (f32[768]{0:T(1024)}, f32[768]{0:T(1024)S(1)}, u32[]{:S(2)}) copy-start(f32[768]{0:T(1024)S(1)} %get-tuple-element.190) | copy-start | bytes 9220
  179.6 6.5 %copy-start.9 = (bf16[512,768]{1,0:T(8,128)(2,1)}, bf16[512,768]{1,0:T(8,128)(2,1)S(1)}, u32[]{:S(2)}) copy-start(bf16[512,768]{1,0:T(8,128)(2,1)S(1)} %get-tuple-element.101) | copy-start | bytes 2359300
  179.6 6.5 %copy-start.12 = (f32[16,8,768]{2,1,0:T(8,128)}, f32[16,8,768]{2,1,0:T(8,128)S(1)}, u32[]{:S(2)}) copy-start(f32[16,8,768]{2,1,0:T(8,128)S(1)} %get-tuple-element.116.si_ref) | copy-start | bytes 1179652
  179.6 6.5 %copy-start.14 = (f32[16,8,768]{2,1,0:T(8,128)}, f32[16,8,768]{2,1,0:T(8,128)S(1)}, u32[]{:S(2)}) copy-start(f32[16,8,768]{2,1,0:T(8,128)S(1)} %get-tuple-element.117.ri_ref) | copy-start | bytes 1179652
  179.7 6.5 %copy-start.30 = (f32[512,768]{1,0:T(8,128)}, f32[512,768]{1,0:T(8,128)S(1)}, u32[]{:S(2)}) copy-start(f32[512,768]{1,0:T(8,128)S(1)} %get-tuple-element.115) | copy-start | bytes 4718596
  179.7 6.5 %copy-start.66 = (f32[128]{0:T(128)S(1)}, f32[128]{0:T(128)}, u32[]{:S(2)}) copy-start(f32[128]{0:T(128)} %param.44) | copy-start | bytes 1540
  179.7 6.5 %copy-start.68 = (f32[128]{0:T(128)S(1)}, f32[128]{0:T(128)}, u32[]{:S(2)}) copy-start(f32[128]{0:T(128)} %param.42) | copy-start | bytes 1540
  179.7 6.4 %copy-start.74 = (f32[128]{0:T(128)S(1)}, f32[128]{0:T(128)}, u32[]{:S(2)}) copy-start(f32[128]{0:T(128)} %param.43) | copy-start | bytes 1540
  179.7 10.7 %copy-start.59 = (bf16[24,16]{0,1:T(8,128)(2,1)S(1)}, bf16[24,16]{0,1:T(8,128)(2,1)}, u32[]{:S(2)}) copy-start(bf16[24,16]{0,1:T(8,128)(2,1)} %param.38) | copy-start | bytes 2308
  189.0 6.6 %collective-permute-start.1 = (bf16[512,128]{1,0:T(8,128)(2,1)}, bf16[512,128]{1,0:T(8,128)(2,1)}, u32[]{:S(2)}, u32[]{:S(2)}) collective-permute-start(bf16[512,128]{1,0:T(8,128)(2,1)} %get-tuple-element.205.refs_0_), channel_id=1, source_target_pairs={{0,8},{8,0},{1,9},{9,1},{2,10},{10,2},{3,11},{11,3},{4,12},{12,4},... | collective-permute-start | bytes 393224 | tf_op jit(solution)/shard_map/ppermute | solution.py:1015
  211.5 16.4 %copy-start.32 = (f32[512,768]{1,0:T(8,128)}, f32[512,768]{1,0:T(8,128)S(1)}, u32[]{:S(2)}) copy-start(f32[512,768]{1,0:T(8,128)S(1)} %get-tuple-element.198) | copy-start | bytes 4718596
  211.8 16.1 %copy-start.60 = (f32[512]{0:T(512)}, f32[512]{0:T(512)S(1)}, u32[]{:S(2)}) copy-start(f32[512]{0:T(512)S(1)} %add_rsqrt_fusion.1) | copy-start | bytes 6148
  221.7 6.2 %copy-start.39 = (f32[512,768]{1,0:T(8,128)}, f32[512,768]{1,0:T(8,128)S(1)}, u32[]{:S(2)}) copy-start(f32[512,768]{1,0:T(8,128)S(1)} %get-tuple-element.222) | copy-start | bytes 4718596
  221.8 6.2 %slice-start = ((s8[6553600]{0:T(1024)(128)(4,1)}), s8[4194304]{0:T(1024)(128)(4,1)S(1)}, s32[]{:S(2)}) async-start(s8[6553600]{0:T(1024)(128)(4,1)} %bitcast.109), calls=%async_computation | async-start | bytes 8388608
  230.7 14.5 %copy-start.45 = (bf16[512,768]{1,0:T(8,128)(2,1)}, bf16[512,768]{1,0:T(8,128)(2,1)S(1)}, u32[]{:S(2)}) copy-start(bf16[512,768]{1,0:T(8,128)(2,1)S(1)} %get-tuple-element.203) | copy-start | bytes 2359300
  235.3 9.8 %copy-start.42 = (bf16[512,1536]{1,0:T(8,128)(2,1)S(1)}, bf16[512,1536]{1,0:T(8,128)(2,1)}, u32[]{:S(2)}) copy-start(bf16[512,1536]{1,0:T(8,128)(2,1)} %copy-done.41) | copy-start | bytes 4718596
  245.0 6.0 %copy-start.47 = (f32[512,128]{1,0:T(8,128)S(1)}, f32[512,128]{1,0:T(8,128)}, u32[]{:S(2)}) copy-start(f32[512,128]{1,0:T(8,128)} %get-tuple-element.110) | copy-start | bytes 786436
  245.1 6.0 %collective-permute-start.3 = (bf16[512,128]{1,0:T(8,128)(2,1)}, bf16[512,128]{1,0:T(8,128)(2,1)S(1)}, u32[]{:S(2)}, u32[]{:S(2)}) collective-permute-start(bf16[512,128]{1,0:T(8,128)(2,1)} %bitcast.128), channel_id=1, source_target_pairs={{0,8},{8,0},{1,9},{9,1},{2,10},{10,2},{3,11},{11,3},{4,12},{12,4},... | collective-permute-start | bytes 393224 | tf_op jit(solution)/shard_map/ppermute | solution.py:1015
  248.1 56.6 %collective-permute-start.4 = (bf16[512,1536]{1,0:T(8,128)(2,1)}, bf16[512,1536]{1,0:T(8,128)(2,1)}, u32[]{:S(2)}, u32[]{:S(2)}) collective-permute-start(bf16[512,1536]{1,0:T(8,128)(2,1)} %bitcast.23), channel_id=1, source_target_pairs={{0,8},{8,0},{1,9},{9,1},{2,10},{10,2},{3,11},{11,3},{4,12},{12,4},... | collective-permute-start | bytes 4718600 | tf_op jit(solution)/shard_map/ppermute | solution.py:1015
  259.3 8.1 %copy-start.13 = (f32[16,8,768]{2,1,0:T(8,128)S(1)}, f32[16,8,768]{2,1,0:T(8,128)}, u32[]{:S(2)}) copy-start(f32[16,8,768]{2,1,0:T(8,128)} %copy-done.12) | copy-start | bytes 1179652
  259.3 8.1 %copy-start.15 = (f32[16,8,768]{2,1,0:T(8,128)S(1)}, f32[16,8,768]{2,1,0:T(8,128)}, u32[]{:S(2)}) copy-start(f32[16,8,768]{2,1,0:T(8,128)} %copy-done.14) | copy-start | bytes 1179652
  267.4 25.8 %collective-permute-start.5 = (f32[16,768]{1,0:T(8,128)}, f32[16,768]{1,0:T(8,128)}, u32[]{:S(2)}, u32[]{:S(2)}) collective-permute-start(f32[16,768]{1,0:T(8,128)} %bitcast.93), channel_id=1, source_target_pairs={{0,8},{8,0},{1,9},{9,1},{2,10},{10,2},{3,11},{11,3},{4,12},{12,4},... | collective-permute-start | bytes 147464 | tf_op jit(solution)/shard_map/ppermute | solution.py:1015
  284.9 7.3 %copy-start.36 = (f32[1,768]{0,1:T(8,128)S(1)}, f32[1,768]{0,1:T(8,128)}, u32[]{:S(2)}) copy-start(f32[1,768]{0,1:T(8,128)} %broadcast_in_dim.62) | copy-start | bytes 9220
  285.0 7.3 %copy-start.37 = (f32[1,768]{0,1:T(8,128)S(1)}, f32[1,768]{0,1:T(8,128)}, u32[]{:S(2)}) copy-start(f32[1,768]{0,1:T(8,128)} %broadcast_in_dim.63) | copy-start | bytes 9220
  285.0 7.3 %copy-start.38 = (f32[33,768]{0,1:T(8,128)S(1)}, f32[33,768]{0,1:T(8,128)}, u32[]{:S(2)}) copy-start(f32[33,768]{0,1:T(8,128)} %copy.91) | copy-start | bytes 304132
  285.0 7.3 %copy-start.75 = (f32[128]{0:T(128)S(1)}, f32[128]{0:T(128)}, u32[]{:S(2)}) copy-start(f32[128]{0:T(128)} %pad.13.clone) | copy-start | bytes 1540
  295.0 9.7 %copy-start.34 = (f32[512,1536]{1,0:T(8,128)S(1)}, f32[512,1536]{1,0:T(8,128)}, u32[]{:S(2)}) copy-start(f32[512,1536]{1,0:T(8,128)} %get-tuple-element.218) | copy-start | bytes 9437188
  423.0 7.0 %copy-start.44 = (bf16[2,2,128,768]{3,2,1,0:T(8,128)(2,1)S(1)}, bf16[2,2,128,768]{3,2,1,0:T(8,128)(2,1)}, u32[]{:S(2)}) copy-start(bf16[2,2,128,768]{3,2,1,0:T(8,128)(2,1)} %get-tuple-element.243) | copy-start | bytes 2359300
  (52 other events, 142.3 us)
